TPU v7x, 32 devices: a whole 2x2x4 slice. The times are simulated.
32 devices in a mesh: gx: 4 (over x, core), gy: 8 (over z, y).
Axes of the slice: x: 2, y: 2, z: 4, core: 2. Of those that a mesh axis runs over, the one named last changes fastest.
Arguments:
- potential: float32 [64, 128, 256], P('gx', 'gy'), may hold values from -1 to 1
- charge: float32 [64, 128, 256], P('gx', 'gy'), may hold values from -6 to 6
- region: int32 [64, 128, 256], P('gx', 'gy'), may hold values from 0 to 16, as said below
- electrode_volts: float32 [16], replicated, may hold values from -2 to 2
Outputs:
- correction: float32 [64, 128, 256], P('gx', 'gy')
Inputs may be any that keep to these rules, and one draw needn't show every extreme that they name: `region`: 0 marks a free cell; k marks a cell of electrode k, held at electrode_volts[k - 1]; about one cell in eight belongs to an electrode.
All inputs are finite; a program needn't handle non-finite values.
Results may differ from a plain program's by a relative error of at most 0.00002.
Values sent between devices are 32-bit elements; how exact they have to be, the bound alone decides.
A program may use at most 64 MiB of HBM per device.

v0:
```python
import jax
import jax.numpy as jnp
from jax import lax
from jax.sharding import PartitionSpec as P

LEVELS = 4
COARSE_SWEEPS = 4


screen = 0.5


def extended(block, sides, width):
    for axis, dim in sides:
        count = lax.axis_size(axis)
        forward = [(i, i + 1) for i in range(count - 1)]
        backward = [(target, source) for source, target in forward]
        low = lax.ppermute(
            lax.slice_in_dim(block, block.shape[dim] - width, None, axis=dim), axis, forward
        )
        high = lax.ppermute(lax.slice_in_dim(block, 0, width, axis=dim), axis, backward)
        block = jnp.concatenate([low, block, high], axis=dim)
    return block


def shifted(block, axis, distance):
    devices = range(lax.axis_size(axis))
    route = [(i - distance, i) for i in devices if i - distance in devices]
    return lax.ppermute(block, axis, route)


def neighbour_sums(padded):
    interior = padded[1:-1, 1:-1]
    flat_sum = padded[2:, 1:-1] + padded[:-2, 1:-1] + padded[1:-1, 2:] + padded[1:-1, :-2]
    padded_z = jnp.pad(interior, ((0, 0), (0, 0), (1, 1)))
    vertical = padded_z[:, :, 2:] + padded_z[:, :, :-2]
    return (flat_sum, vertical)


def checker(span_x, span_y, span_z):
    index_x = jnp.arange(span_x, dtype=jnp.int32)[:, None, None]
    index_y = jnp.arange(span_y, dtype=jnp.int32)[None, :, None]
    index_z = jnp.arange(span_z, dtype=jnp.int32)[None, None, :]
    return (index_x + index_y + index_z) % 2


def whole_rims(iterate, wanted):
    return extended(iterate, (("gx", 0), ("gy", 1)), 1)


def half_sweep(iterate, source, divisor, weight, movable, colour, padder):
    flat_sum, vertical = neighbour_sums(padder(iterate, 1 - colour))
    renewed = (source + weight * flat_sum + vertical) / divisor
    span_x, span_y, span_z = iterate.shape
    update = checker(span_x, span_y, span_z) == colour
    if movable is not None:
        update = jnp.logical_and(update, movable)
    return jnp.where(update, renewed, iterate)


def full_sweep(iterate, source, divisor, weight, movable, padder):
    iterate = half_sweep(iterate, source, divisor, weight, movable, 0, padder)
    return half_sweep(iterate, source, divisor, weight, movable, 1, padder)


def restrict(values):
    paired = values.reshape(values.shape[0] // 2, 2, values.shape[1], values.shape[2])
    even_rows, odd_rows = (paired[:, 0], paired[:, 1])
    from_below = shifted(odd_rows[-1:], "gx", 1)
    before = jnp.concatenate([from_below, odd_rows[:-1]], axis=0)
    across = 0.25 * before + 0.5 * even_rows + 0.25 * odd_rows
    paired = across.reshape(across.shape[0], across.shape[1] // 2, 2, across.shape[2])
    even_rows, odd_rows = (paired[:, :, 0], paired[:, :, 1])
    from_below = shifted(odd_rows[:, -1:], "gy", 1)
    before = jnp.concatenate([from_below, odd_rows[:, :-1]], axis=1)
    return 0.25 * before + 0.5 * even_rows + 0.25 * odd_rows


def coarsen(values):
    paired = values.reshape(values.shape[0] // 2, 2, values.shape[1], values.shape[2])
    across = 0.5 * (paired[:, 0] + paired[:, 1])
    paired = across.reshape(across.shape[0], across.shape[1] // 2, 2, across.shape[2])
    return 0.5 * (paired[:, :, 0] + paired[:, :, 1])


def coarsest_solve(source, coefficient, weight, padder):
    divisor = 4.0 * weight + 2.0 + coefficient
    iterate = jnp.zeros_like(source)
    for sweep_index in range(COARSE_SWEEPS):
        iterate = full_sweep(iterate, source, divisor, weight, None, padder)
    return iterate


def solve_level(grid_level, source, coefficient, iterate, movable, padder):
    weight = 0.25**grid_level
    if grid_level == LEVELS - 1:
        return coarsest_solve(source, coefficient, weight, padder)
    divisor = 4.0 * weight + 2.0 + coefficient
    iterate = full_sweep(iterate, source, divisor, weight, movable, padder)
    flat_sum, vertical = neighbour_sums(whole_rims(iterate, 0))
    residual = source - (divisor * iterate - (weight * flat_sum + vertical))
    if movable is not None:
        residual = jnp.where(movable, residual, 0.0)
    coarse_source = restrict(residual)
    coarse_coefficient = coarsen(coefficient)
    coarse = solve_level(
        grid_level + 1,
        coarse_source,
        coarse_coefficient,
        jnp.zeros_like(coarse_source),
        None,
        padder,
    )
    lifted = jnp.repeat(jnp.repeat(coarse, 2, axis=0), 2, axis=1)
    if movable is not None:
        lifted = jnp.where(movable, lifted, 0.0)
    iterate = iterate + lifted
    iterate = full_sweep(iterate, source, divisor, weight, movable, padder)
    return iterate


def body(potential, charge, region, electrode_volts):
    movable = region == 0
    dirichlet = jnp.zeros_like(potential)
    for electrode in range(electrode_volts.shape[0]):
        dirichlet = dirichlet + jnp.where(
            region == electrode + 1, electrode_volts[electrode], jnp.float32(0.0)
        )
    flat_sum, vertical = neighbour_sums(whole_rims(potential, 0))
    source = (
        charge - (6.0 * potential - (flat_sum + vertical)) - screen * (jnp.exp(potential) - 1.0)
    )
    coefficient = screen * jnp.exp(potential)
    return solve_level(0, source, coefficient, dirichlet, movable, whole_rims)


def solution(mesh):
    placed = (P("gx", "gy", None), P("gx", "gy", None), P("gx", "gy", None), P())
    return jax.shard_map(
        body, mesh=mesh, in_specs=placed, out_specs=P("gx", "gy", None), check_vma=False
    )
```

profile of v0, /device:TPU:1, one launch (start us, length us, event | category | flops | bytes accessed | tf_op | source)
XLA Modules:
  0.0 392.8 jit_solution(6413428129334735633)
XLA Ops:
  2.0 11.3 %select_add_fusion.1 = f32[16,16,256]{2,1,0:T(8,128)S(1)} fusion(s32[16,16,256]{2,1,0:T(8,128)} %param.6, f32[]{:T(128)} %bitcast.15, f32[]{:T(128)} %bitcast.14, f32[]{:T(128)} %bitcast.13, f32[]{:T(128)} %bitcast.12, f32[]{:T(128)} %bitcast.11, f32[]{:T(128)} %bitcast.10, f32[]{:T(128)} %bitcast.9, f32[]{:T(128)} %bitcast.8, f32[]{:T(128)} %bitcast.7, ...), kind=kLoop, calls=%fused_computation.109 | loop fusion | flops 3080192 | bytes 524352 | tf_op jit(solution)/shard_map/add | solution.py:126
  48.6 5.2 %collective-permute-start.11 = (f32[18,1,256]{2,1,0:T(1,128)S(1)}, f32[18,1,256]{2,1,0:T(1,128)S(1)}, u32[]{:S(2)}, u32[]{:S(2)}) collective-permute-start(f32[18,1,256]{2,1,0:T(1,128)S(1)} %get-tuple-element.24), channel_id=1, source_target_pairs={{0,1},{1,2},{2,3},{3,4},{4,5},{5,6},{6,7},{8,9},{9,10},{10,11},{11... | collective-permute-start | bytes 55304 | tf_op jit(solution)/shard_map/ppermute | solution.py:18
  68.4 5.5 %collective-permute-start.15 = (f32[18,1,256]{2,1,0:T(1,128)S(1)}, f32[18,1,256]{2,1,0:T(1,128)S(1)}, u32[]{:S(2)}, u32[]{:S(2)}) collective-permute-start(f32[18,1,256]{2,1,0:T(1,128)S(1)} %get-tuple-element.22), channel_id=1, source_target_pairs={{0,1},{1,2},{2,3},{3,4},{4,5},{5,6},{6,7},{8,9},{9,10},{10,11},{11... | collective-permute-start | bytes 55304 | tf_op jit(solution)/shard_map/ppermute | solution.py:18
  75.2 4.9 %collective-permute-start.21 = (f32[10,1,256]{2,1,0:T(1,128)S(1)}, f32[10,1,256]{2,1,0:T(1,128)S(1)}, u32[]{:S(2)}, u32[]{:S(2)}) collective-permute-start(f32[10,1,256]{2,1,0:T(1,128)S(1)} %get-tuple-element.58), channel_id=1, source_target_pairs={{0,1},{1,2},{2,3},{3,4},{4,5},{5,6},{6,7},{8,9},{9,10},{10,11},{11... | collective-permute-start | bytes 30728 | tf_op jit(solution)/shard_map/ppermute | solution.py:18
  89.8 5.1 %collective-permute-start.23 = (f32[1,8,256]{2,1,0:T(8,128)S(1)}, f32[1,8,256]{2,1,0:T(8,128)S(1)}, u32[]{:S(2)}, u32[]{:S(2)}) collective-permute-start(f32[1,8,256]{2,1,0:T(8,128)S(1)} %get-tuple-element.67), channel_id=1, source_target_pairs={{0,8},{8,16},{16,24},{1,9},{9,17},{17,25},{2,10},{10,18},{18,26},{... | collective-permute-start | bytes 24584 | tf_op jit(solution)/shard_map/ppermute | solution.py:18
  124.0 4.9 %collective-permute-start.29 = (f32[10,1,256]{2,1,0:T(1,128)S(1)}, f32[10,1,256]{2,1,0:T(1,128)S(1)}, u32[]{:S(2)}, u32[]{:S(2)}) collective-permute-start(f32[10,1,256]{2,1,0:T(1,128)S(1)} %get-tuple-element.54), channel_id=1, source_target_pairs={{0,1},{1,2},{2,3},{3,4},{4,5},{5,6},{6,7},{8,9},{9,10},{10,11},{11... | collective-permute-start | bytes 30728 | tf_op jit(solution)/shard_map/ppermute | solution.py:18
  142.2 5.0 %collective-permute-start.37 = (f32[1,4,256]{2,1,0:T(4,128)S(1)}, f32[1,4,256]{2,1,0:T(4,128)S(1)}, u32[]{:S(2)}, u32[]{:S(2)}) collective-permute-start(f32[1,4,256]{2,1,0:T(4,128)S(1)} %get-tuple-element.93), channel_id=1, source_target_pairs={{0,8},{8,16},{16,24},{1,9},{9,17},{17,25},{2,10},{10,18},{18,26},{... | collective-permute-start | bytes 12296 | tf_op jit(solution)/shard_map/ppermute | solution.py:18
  164.9 5.2 %collective-permute-start.49 = (f32[4,1,256]{2,1,0:T(1,128)S(1)}, f32[4,1,256]{2,1,0:T(1,128)S(1)}, u32[]{:S(2)}, u32[]{:S(2)}) collective-permute-start(f32[4,1,256]{2,1,0:T(1,128)S(1)} %get-tuple-element.114), channel_id=1, source_target_pairs={{0,1},{1,2},{2,3},{3,4},{4,5},{5,6},{6,7},{8,9},{9,10},{10,11},{11... | collective-permute-start | bytes 12296 | tf_op jit(solution)/shard_map/ppermute | solution.py:18
  171.4 5.4 %collective-permute-start.43 = (f32[6,1,256]{2,1,0:T(1,128)S(1)}, f32[6,1,256]{2,1,0:T(1,128)S(1)}, u32[]{:S(2)}, u32[]{:S(2)}) collective-permute-start(f32[6,1,256]{2,1,0:T(1,128)S(1)} %get-tuple-element.78), channel_id=1, source_target_pairs={{0,1},{1,2},{2,3},{3,4},{4,5},{5,6},{6,7},{8,9},{9,10},{10,11},{11... | collective-permute-start | bytes 18440 | tf_op jit(solution)/shard_map/ppermute | solution.py:18
  177.7 4.8 %collective-permute-start.44 = (f32[1,4,256]{2,1,0:T(4,128)S(1)}, f32[1,4,256]{2,1,0:T(4,128)S(1)}, u32[]{:S(2)}, u32[]{:S(2)}) collective-permute-start(f32[1,4,256]{2,1,0:T(4,128)S(1)} %get-tuple-element.87), channel_id=1, source_target_pairs={{0,8},{8,16},{16,24},{1,9},{9,17},{17,25},{2,10},{10,18},{18,26},{... | collective-permute-start | bytes 12296 | tf_op jit(solution)/shard_map/ppermute | solution.py:29
  188.7 5.0 %collective-permute-start.51 = (f32[1,2,256]{2,1,0:T(2,128)S(1)}, f32[1,2,256]{2,1,0:T(2,128)S(1)}, u32[]{:S(2)}, u32[]{:S(2)}) collective-permute-start(f32[1,2,256]{2,1,0:T(2,128)S(1)} %get-tuple-element.127), channel_id=1, source_target_pairs={{0,8},{8,16},{16,24},{1,9},{9,17},{17,25},{2,10},{10,18},{18,26},{... | collective-permute-start | bytes 6152 | tf_op jit(solution)/shard_map/ppermute | solution.py:18
  200.0 5.4 %collective-permute-start.53 = (f32[4,1,256]{2,1,0:T(1,128)S(1)}, f32[4,1,256]{2,1,0:T(1,128)S(1)}, u32[]{:S(2)}, u32[]{:S(2)}) collective-permute-start(f32[4,1,256]{2,1,0:T(1,128)S(1)} %get-tuple-element.108), channel_id=1, source_target_pairs={{0,1},{1,2},{2,3},{3,4},{4,5},{5,6},{6,7},{8,9},{9,10},{10,11},{11... | collective-permute-start | bytes 12296 | tf_op jit(solution)/shard_map/ppermute | solution.py:18
  215.3 5.4 %collective-permute-start.57 = (f32[4,1,256]{2,1,0:T(1,128)S(1)}, f32[4,1,256]{2,1,0:T(1,128)S(1)}, u32[]{:S(2)}, u32[]{:S(2)}) collective-permute-start(f32[4,1,256]{2,1,0:T(1,128)S(1)} %get-tuple-element.106), channel_id=1, source_target_pairs={{0,1},{1,2},{2,3},{3,4},{4,5},{5,6},{6,7},{8,9},{9,10},{10,11},{11... | collective-permute-start | bytes 12296 | tf_op jit(solution)/shard_map/ppermute | solution.py:18
  230.6 5.4 %collective-permute-start.61 = (f32[4,1,256]{2,1,0:T(1,128)S(1)}, f32[4,1,256]{2,1,0:T(1,128)S(1)}, u32[]{:S(2)}, u32[]{:S(2)}) collective-permute-start(f32[4,1,256]{2,1,0:T(1,128)S(1)} %get-tuple-element.104), channel_id=1, source_target_pairs={{0,1},{1,2},{2,3},{3,4},{4,5},{5,6},{6,7},{8,9},{9,10},{10,11},{11... | collective-permute-start | bytes 12296 | tf_op jit(solution)/shard_map/ppermute | solution.py:18
  245.9 5.4 %collective-permute-start.65 = (f32[4,1,256]{2,1,0:T(1,128)S(1)}, f32[4,1,256]{2,1,0:T(1,128)S(1)}, u32[]{:S(2)}, u32[]{:S(2)}) collective-permute-start(f32[4,1,256]{2,1,0:T(1,128)S(1)} %get-tuple-element.102), channel_id=1, source_target_pairs={{0,1},{1,2},{2,3},{3,4},{4,5},{5,6},{6,7},{8,9},{9,10},{10,11},{11... | collective-permute-start | bytes 12296 | tf_op jit(solution)/shard_map/ppermute | solution.py:18
  261.2 5.4 %collective-permute-start.69 = (f32[4,1,256]{2,1,0:T(1,128)S(1)}, f32[4,1,256]{2,1,0:T(1,128)S(1)}, u32[]{:S(2)}, u32[]{:S(2)}) collective-permute-start(f32[4,1,256]{2,1,0:T(1,128)S(1)} %get-tuple-element.100), channel_id=1, source_target_pairs={{0,1},{1,2},{2,3},{3,4},{4,5},{5,6},{6,7},{8,9},{9,10},{10,11},{11... | collective-permute-start | bytes 12296 | tf_op jit(solution)/shard_map/ppermute | solution.py:18
  276.5 5.4 %collective-permute-start.73 = (f32[4,1,256]{2,1,0:T(1,128)S(1)}, f32[4,1,256]{2,1,0:T(1,128)S(1)}, u32[]{:S(2)}, u32[]{:S(2)}) collective-permute-start(f32[4,1,256]{2,1,0:T(1,128)S(1)} %get-tuple-element.98), channel_id=1, source_target_pairs={{0,1},{1,2},{2,3},{3,4},{4,5},{5,6},{6,7},{8,9},{9,10},{10,11},{11... | collective-permute-start | bytes 12296 | tf_op jit(solution)/shard_map/ppermute | solution.py:18
  291.8 5.4 %collective-permute-start.77 = (f32[4,1,256]{2,1,0:T(1,128)S(1)}, f32[4,1,256]{2,1,0:T(1,128)S(1)}, u32[]{:S(2)}, u32[]{:S(2)}) collective-permute-start(f32[4,1,256]{2,1,0:T(1,128)S(1)} %get-tuple-element.96), channel_id=1, source_target_pairs={{0,1},{1,2},{2,3},{3,4},{4,5},{5,6},{6,7},{8,9},{9,10},{10,11},{11... | collective-permute-start | bytes 12296 | tf_op jit(solution)/shard_map/ppermute | solution.py:18
  307.2 5.4 %collective-permute-start.81 = (f32[6,1,256]{2,1,0:T(1,128)S(1)}, f32[6,1,256]{2,1,0:T(1,128)S(1)}, u32[]{:S(2)}, u32[]{:S(2)}) collective-permute-start(f32[6,1,256]{2,1,0:T(1,128)S(1)} %get-tuple-element.76), channel_id=1, source_target_pairs={{0,1},{1,2},{2,3},{3,4},{4,5},{5,6},{6,7},{8,9},{9,10},{10,11},{11... | collective-permute-start | bytes 18440 | tf_op jit(solution)/shard_map/ppermute | solution.py:18
  322.6 5.4 %collective-permute-start.85 = (f32[6,1,256]{2,1,0:T(1,128)S(1)}, f32[6,1,256]{2,1,0:T(1,128)S(1)}, u32[]{:S(2)}, u32[]{:S(2)}) collective-permute-start(f32[6,1,256]{2,1,0:T(1,128)S(1)} %get-tuple-element.74), channel_id=1, source_target_pairs={{0,1},{1,2},{2,3},{3,4},{4,5},{5,6},{6,7},{8,9},{9,10},{10,11},{11... | collective-permute-start | bytes 18440 | tf_op jit(solution)/shard_map/ppermute | solution.py:18
  338.1 5.4 %collective-permute-start.89 = (f32[10,1,256]{2,1,0:T(1,128)S(1)}, f32[10,1,256]{2,1,0:T(1,128)S(1)}, u32[]{:S(2)}, u32[]{:S(2)}) collective-permute-start(f32[10,1,256]{2,1,0:T(1,128)S(1)} %get-tuple-element.52), channel_id=1, source_target_pairs={{0,1},{1,2},{2,3},{3,4},{4,5},{5,6},{6,7},{8,9},{9,10},{10,11},{11... | collective-permute-start | bytes 30728 | tf_op jit(solution)/shard_map/ppermute | solution.py:18
  353.6 5.4 %collective-permute-start.93 = (f32[10,1,256]{2,1,0:T(1,128)S(1)}, f32[10,1,256]{2,1,0:T(1,128)S(1)}, u32[]{:S(2)}, u32[]{:S(2)}) collective-permute-start(f32[10,1,256]{2,1,0:T(1,128)S(1)} %get-tuple-element.50), channel_id=1, source_target_pairs={{0,1},{1,2},{2,3},{3,4},{4,5},{5,6},{6,7},{8,9},{9,10},{10,11},{11... | collective-permute-start | bytes 30728 | tf_op jit(solution)/shard_map/ppermute | solution.py:18
  369.5 5.4 %collective-permute-start.97 = (f32[18,1,256]{2,1,0:T(1,128)S(1)}, f32[18,1,256]{2,1,0:T(1,128)S(1)}, u32[]{:S(2)}, u32[]{:S(2)}) collective-permute-start(f32[18,1,256]{2,1,0:T(1,128)S(1)} %get-tuple-element.20), channel_id=1, source_target_pairs={{0,1},{1,2},{2,3},{3,4},{4,5},{5,6},{6,7},{8,9},{9,10},{10,11},{11... | collective-permute-start | bytes 55304 | tf_op jit(solution)/shard_map/ppermute | solution.py:18
  385.4 5.4 %collective-permute-start.101 = (f32[18,1,256]{2,1,0:T(1,128)S(1)}, f32[18,1,256]{2,1,0:T(1,128)S(1)}, u32[]{:S(2)}, u32[]{:S(2)}) collective-permute-start(f32[18,1,256]{2,1,0:T(1,128)S(1)} %get-tuple-element.18), channel_id=1, source_target_pairs={{0,1},{1,2},{2,3},{3,4},{4,5},{5,6},{6,7},{8,9},{9,10},{10,11},{11... | collective-permute-start | bytes 55304 | tf_op jit(solution)/shard_map/ppermute | solution.py:18
  (330 shorter events, 257.9 us)
Async XLA Ops:
  13.2 12.0 %collective-permute-start.5 = (f32[1,16,256]{2,1,0:T(8,128)S(1)}, f32[1,16,256]{2,1,0:T(8,128)S(1)}, u32[]{:S(2)}, u32[]{:S(2)}) collective-permute-start(f32[1,16,256]{2,1,0:T(8,128)S(1)} %get-tuple-element.43), channel_id=1, source_target_pairs={{0,8},{8,16},{16,24},{1,9},{9,17},{17,25},{2,10},{10,18},{18,26},{... | collective-permute-start | bytes 49160 | tf_op jit(solution)/shard_map/ppermute | solution.py:18
  19.7 11.0 %collective-permute-start = (f32[1,16,256]{2,1,0:T(8,128)S(1)}, f32[1,16,256]{2,1,0:T(8,128)S(1)}, u32[]{:S(2)}, u32[]{:S(2)}) collective-permute-start(f32[1,16,256]{2,1,0:T(8,128)S(1)} %get-tuple-element.41), channel_id=1, source_target_pairs={{8,0},{16,8},{24,16},{9,1},{17,9},{25,17},{10,2},{18,10},{26,18},{... | collective-permute-start | bytes 49160 | tf_op jit(solution)/shard_map/ppermute | solution.py:21
  21.6 9.0 %collective-permute-start.1 = (f32[1,16,256]{2,1,0:T(8,128)S(1)}, f32[1,16,256]{2,1,0:T(8,128)S(1)}, u32[]{:S(2)}, u32[]{:S(2)}) collective-permute-start(f32[1,16,256]{2,1,0:T(8,128)S(1)} %get-tuple-element.42), channel_id=1, source_target_pairs={{0,8},{8,16},{16,24},{1,9},{9,17},{17,25},{2,10},{10,18},{18,26},{... | collective-permute-start | bytes 49160 | tf_op jit(solution)/shard_map/ppermute | solution.py:18
  25.3 11.6 %collective-permute-start.6 = (f32[18,1,256]{2,1,0:T(1,128)S(1)}, f32[18,1,256]{2,1,0:T(1,128)S(1)}, u32[]{:S(2)}, u32[]{:S(2)}) collective-permute-start(f32[18,1,256]{2,1,0:T(1,128)S(1)} %get-tuple-element.27), channel_id=1, source_target_pairs={{1,0},{2,1},{3,2},{4,3},{5,4},{6,5},{7,6},{9,8},{10,9},{11,10},{12... | collective-permute-start | bytes 55304 | tf_op jit(solution)/shard_map/ppermute | solution.py:21
  26.6 10.3 %collective-permute-start.7 = (f32[18,1,256]{2,1,0:T(1,128)S(1)}, f32[18,1,256]{2,1,0:T(1,128)S(1)}, u32[]{:S(2)}, u32[]{:S(2)}) collective-permute-start(f32[18,1,256]{2,1,0:T(1,128)S(1)} %get-tuple-element.28), channel_id=1, source_target_pairs={{0,1},{1,2},{2,3},{3,4},{4,5},{5,6},{6,7},{8,9},{9,10},{10,11},{11... | collective-permute-start | bytes 55304 | tf_op jit(solution)/shard_map/ppermute | solution.py:18
  47.3 10.8 %collective-permute-start.10 = (f32[18,1,256]{2,1,0:T(1,128)S(1)}, f32[18,1,256]{2,1,0:T(1,128)S(1)}, u32[]{:S(2)}, u32[]{:S(2)}) collective-permute-start(f32[18,1,256]{2,1,0:T(1,128)S(1)} %get-tuple-element.23), channel_id=1, source_target_pairs={{1,0},{2,1},{3,2},{4,3},{5,4},{6,5},{7,6},{9,8},{10,9},{11,10},{12... | collective-permute-start | bytes 55304 | tf_op jit(solution)/shard_map/ppermute | solution.py:21
  48.6 9.5 %collective-permute-start.11 = (f32[18,1,256]{2,1,0:T(1,128)S(1)}, f32[18,1,256]{2,1,0:T(1,128)S(1)}, u32[]{:S(2)}, u32[]{:S(2)}) collective-permute-start(f32[18,1,256]{2,1,0:T(1,128)S(1)} %get-tuple-element.24), channel_id=1, source_target_pairs={{0,1},{1,2},{2,3},{3,4},{4,5},{5,6},{6,7},{8,9},{9,10},{10,11},{11... | collective-permute-start | bytes 55304 | tf_op jit(solution)/shard_map/ppermute | solution.py:18
  53.8 20.1 %collective-permute-start.19 = (f32[1,8,256]{2,1,0:T(8,128)S(1)}, f32[1,8,256]{2,1,0:T(8,128)S(1)}, u32[]{:S(2)}, u32[]{:S(2)}) collective-permute-start(f32[1,8,256]{2,1,0:T(8,128)S(1)} %broadcast.274), channel_id=1, source_target_pairs={{0,8},{8,16},{16,24},{1,9},{9,17},{17,25},{2,10},{10,18},{18,26},{... | collective-permute-start | bytes 24584 | tf_op jit(solution)/shard_map/ppermute | solution.py:18
  56.0 17.9 %collective-permute-start.18 = (f32[1,8,256]{2,1,0:T(8,128)S(1)}, f32[1,8,256]{2,1,0:T(8,128)S(1)}, u32[]{:S(2)}, u32[]{:S(2)}) collective-permute-start(f32[1,8,256]{2,1,0:T(8,128)S(1)} %broadcast.274), channel_id=1, source_target_pairs={{8,0},{16,8},{24,16},{9,1},{17,9},{25,17},{10,2},{18,10},{26,18},{... | collective-permute-start | bytes 24584 | tf_op jit(solution)/shard_map/ppermute | solution.py:21
  67.1 13.0 %collective-permute-start.14 = (f32[18,1,256]{2,1,0:T(1,128)S(1)}, f32[18,1,256]{2,1,0:T(1,128)S(1)}, u32[]{:S(2)}, u32[]{:S(2)}) collective-permute-start(f32[18,1,256]{2,1,0:T(1,128)S(1)} %get-tuple-element.21), channel_id=1, source_target_pairs={{1,0},{2,1},{3,2},{4,3},{5,4},{6,5},{7,6},{9,8},{10,9},{11,10},{12... | collective-permute-start | bytes 55304 | tf_op jit(solution)/shard_map/ppermute | solution.py:21
  68.4 11.7 %collective-permute-start.15 = (f32[18,1,256]{2,1,0:T(1,128)S(1)}, f32[18,1,256]{2,1,0:T(1,128)S(1)}, u32[]{:S(2)}, u32[]{:S(2)}) collective-permute-start(f32[18,1,256]{2,1,0:T(1,128)S(1)} %get-tuple-element.22), channel_id=1, source_target_pairs={{0,1},{1,2},{2,3},{3,4},{4,5},{5,6},{6,7},{8,9},{9,10},{10,11},{11... | collective-permute-start | bytes 55304 | tf_op jit(solution)/shard_map/ppermute | solution.py:18
  73.9 15.1 %collective-permute-start.20 = (f32[10,1,256]{2,1,0:T(1,128)S(1)}, f32[10,1,256]{2,1,0:T(1,128)S(1)}, u32[]{:S(2)}, u32[]{:S(2)}) collective-permute-start(f32[10,1,256]{2,1,0:T(1,128)S(1)} %get-tuple-element.57), channel_id=1, source_target_pairs={{1,0},{2,1},{3,2},{4,3},{5,4},{6,5},{7,6},{9,8},{10,9},{11,10},{12... | collective-permute-start | bytes 30728 | tf_op jit(solution)/shard_map/ppermute | solution.py:21
  75.2 13.8 %collective-permute-start.21 = (f32[10,1,256]{2,1,0:T(1,128)S(1)}, f32[10,1,256]{2,1,0:T(1,128)S(1)}, u32[]{:S(2)}, u32[]{:S(2)}) collective-permute-start(f32[10,1,256]{2,1,0:T(1,128)S(1)} %get-tuple-element.58), channel_id=1, source_target_pairs={{0,1},{1,2},{2,3},{3,4},{4,5},{5,6},{6,7},{8,9},{9,10},{10,11},{11... | collective-permute-start | bytes 30728 | tf_op jit(solution)/shard_map/ppermute | solution.py:18
  89.8 16.2 %collective-permute-start.23 = (f32[1,8,256]{2,1,0:T(8,128)S(1)}, f32[1,8,256]{2,1,0:T(8,128)S(1)}, u32[]{:S(2)}, u32[]{:S(2)}) collective-permute-start(f32[1,8,256]{2,1,0:T(8,128)S(1)} %get-tuple-element.67), channel_id=1, source_target_pairs={{0,8},{8,16},{16,24},{1,9},{9,17},{17,25},{2,10},{10,18},{18,26},{... | collective-permute-start | bytes 24584 | tf_op jit(solution)/shard_map/ppermute | solution.py:18
  94.9 11.2 %collective-permute-start.22 = (f32[1,8,256]{2,1,0:T(8,128)S(1)}, f32[1,8,256]{2,1,0:T(8,128)S(1)}, u32[]{:S(2)}, u32[]{:S(2)}) collective-permute-start(f32[1,8,256]{2,1,0:T(8,128)S(1)} %get-tuple-element.68), channel_id=1, source_target_pairs={{8,0},{16,8},{24,16},{9,1},{17,9},{25,17},{10,2},{18,10},{26,18},{... | collective-permute-start | bytes 24584 | tf_op jit(solution)/shard_map/ppermute | solution.py:21
  96.8 61.2 %collective-permute-start.47 = (f32[1,2,256]{2,1,0:T(2,128)S(1)}, f32[1,2,256]{2,1,0:T(2,128)S(1)}, u32[]{:S(2)}, u32[]{:S(2)}) collective-permute-start(f32[1,2,256]{2,1,0:T(2,128)S(1)} %broadcast.289), channel_id=1, source_target_pairs={{0,8},{8,16},{16,24},{1,9},{9,17},{17,25},{2,10},{10,18},{18,26},{... | collective-permute-start | bytes 6152 | tf_op jit(solution)/shard_map/ppermute | solution.py:18
  100.5 57.5 %collective-permute-start.46 = (f32[1,2,256]{2,1,0:T(2,128)S(1)}, f32[1,2,256]{2,1,0:T(2,128)S(1)}, u32[]{:S(2)}, u32[]{:S(2)}) collective-permute-start(f32[1,2,256]{2,1,0:T(2,128)S(1)} %broadcast.289), channel_id=1, source_target_pairs={{8,0},{16,8},{24,16},{9,1},{17,9},{25,17},{10,2},{18,10},{26,18},{... | collective-permute-start | bytes 6152 | tf_op jit(solution)/shard_map/ppermute | solution.py:21
  102.4 15.3 %collective-permute-start.33 = (f32[1,4,256]{2,1,0:T(4,128)S(1)}, f32[1,4,256]{2,1,0:T(4,128)S(1)}, u32[]{:S(2)}, u32[]{:S(2)}) collective-permute-start(f32[1,4,256]{2,1,0:T(4,128)S(1)} %broadcast.281), channel_id=1, source_target_pairs={{0,8},{8,16},{16,24},{1,9},{9,17},{17,25},{2,10},{10,18},{18,26},{... | collective-permute-start | bytes 12296 | tf_op jit(solution)/shard_map/ppermute | solution.py:18
  119.7 21.7 %collective-permute-start.34 = (f32[6,1,256]{2,1,0:T(1,128)S(1)}, f32[6,1,256]{2,1,0:T(1,128)S(1)}, u32[]{:S(2)}, u32[]{:S(2)}) collective-permute-start(f32[6,1,256]{2,1,0:T(1,128)S(1)} %get-tuple-element.81), channel_id=1, source_target_pairs={{1,0},{2,1},{3,2},{4,3},{5,4},{6,5},{7,6},{9,8},{10,9},{11,10},{12... | collective-permute-start | bytes 18440 | tf_op jit(solution)/shard_map/ppermute | solution.py:21
  124.0 9.2 %collective-permute-start.29 = (f32[10,1,256]{2,1,0:T(1,128)S(1)}, f32[10,1,256]{2,1,0:T(1,128)S(1)}, u32[]{:S(2)}, u32[]{:S(2)}) collective-permute-start(f32[10,1,256]{2,1,0:T(1,128)S(1)} %get-tuple-element.54), channel_id=1, source_target_pairs={{0,1},{1,2},{2,3},{3,4},{4,5},{5,6},{6,7},{8,9},{9,10},{10,11},{11... | collective-permute-start | bytes 30728 | tf_op jit(solution)/shard_map/ppermute | solution.py:18
  128.9 12.4 %collective-permute-start.35 = (f32[6,1,256]{2,1,0:T(1,128)S(1)}, f32[6,1,256]{2,1,0:T(1,128)S(1)}, u32[]{:S(2)}, u32[]{:S(2)}) collective-permute-start(f32[6,1,256]{2,1,0:T(1,128)S(1)} %get-tuple-element.82), channel_id=1, source_target_pairs={{0,1},{1,2},{2,3},{3,4},{4,5},{5,6},{6,7},{8,9},{9,10},{10,11},{11... | collective-permute-start | bytes 18440 | tf_op jit(solution)/shard_map/ppermute | solution.py:18
  158.9 11.2 %collective-permute-start.41 = (f32[1,4,256]{2,1,0:T(4,128)S(1)}, f32[1,4,256]{2,1,0:T(4,128)S(1)}, u32[]{:S(2)}, u32[]{:S(2)}) collective-permute-start(f32[1,4,256]{2,1,0:T(4,128)S(1)} %get-tuple-element.91), channel_id=1, source_target_pairs={{0,8},{8,16},{16,24},{1,9},{9,17},{17,25},{2,10},{10,18},{18,26},{... | collective-permute-start | bytes 12296 | tf_op jit(solution)/shard_map/ppermute | solution.py:18
  163.6 24.3 %collective-permute-start.48 = (f32[4,1,256]{2,1,0:T(1,128)S(1)}, f32[4,1,256]{2,1,0:T(1,128)S(1)}, u32[]{:S(2)}, u32[]{:S(2)}) collective-permute-start(f32[4,1,256]{2,1,0:T(1,128)S(1)} %get-tuple-element.113), channel_id=1, source_target_pairs={{1,0},{2,1},{3,2},{4,3},{5,4},{6,5},{7,6},{9,8},{10,9},{11,10},{12... | collective-permute-start | bytes 12296 | tf_op jit(solution)/shard_map/ppermute | solution.py:21
  164.9 23.0 %collective-permute-start.49 = (f32[4,1,256]{2,1,0:T(1,128)S(1)}, f32[4,1,256]{2,1,0:T(1,128)S(1)}, u32[]{:S(2)}, u32[]{:S(2)}) collective-permute-start(f32[4,1,256]{2,1,0:T(1,128)S(1)} %get-tuple-element.114), channel_id=1, source_target_pairs={{0,1},{1,2},{2,3},{3,4},{4,5},{5,6},{6,7},{8,9},{9,10},{10,11},{11... | collective-permute-start | bytes 12296 | tf_op jit(solution)/shard_map/ppermute | solution.py:18
  (81 other events, 480.0 us)
where the time goes:
time: 400 us; the launch traced here: 393 us
  starting transfers between devices  305 us (76%)
  waiting for transfers between devices  66 us (16%)
  other arithmetic  16.5 us (4%)
    ppermute x48, starting transfers between devices, extended(): lax.ppermute(lax.slice_in_dim(block, block.shape[dim] - width, None, axis...  204 us
    ppermute x48, starting transfers between devices, extended(): lax.ppermute(lax.slice_in_dim(block, 0, width, axis=dim), axis, backward)  77.4 us
    ppermute x48, waiting for transfers between devices, extended(): lax.ppermute(lax.slice_in_dim(block, 0, width, axis=dim), axis, backward)  50 us
    ppermute x6, starting transfers between devices, shifted(): return lax.ppermute(block, axis, route)  23.7 us
    ppermute x48, waiting for transfers between devices, extended(): lax.ppermute(lax.slice_in_dim(block, block.shape[dim] - width, None, axis...  12.2 us
    add x1, other arithmetic, body(): dirichlet + jnp.where(region == electrode + 1, electrode_volts[electrode]...  11.3 us
  transfers between devices with their start and end apart: 102, of which 39 were waited for; matrix products, arithmetic and copies ran while one was open for 1% of the time, Pallas kernels for 0%

commit v1 on v0

v1 whole, which is shorter than its diff:
```python
import functools

import jax
import jax.numpy as jnp
from jax import lax
from jax.experimental import pallas as pl
from jax.experimental.pallas import tpu as pltpu
from jax.sharding import PartitionSpec as P

MESH = pl.DeviceIdType.MESH
COARSE_SWEEPS = 4
REACH = 5

FACES = ((1, 0), (-1, 0), (0, 1), (0, -1))
AROUND = FACES + ((1, 1), (1, -1), (-1, 1), (-1, -1))
LOW_FACES = ((1, 0), (0, 1), (1, 1))
LOW_DEEP = FACES + ((1, 1), (1, -1), (-1, 1))


def cut(n, d, low, high):
    first, last = max(0, n * d - low), min(n, n * d + n + high)
    return first, first - n * d, last - first


def kernel(
    gx, gy, win_x, win_y,
    potential, charge, region, volts, out,
    pot, start, first, delta, reg, inv1, src1, inv2, src2, gat_i, gat_s, inv3, src3, e3, lift2, lift1, u0, u1, u2,
    send_sem, recv_sem, gsend_i, grecv_i, gsend_s, grecv_s,
):
    mx, my = lax.axis_index("gx"), lax.axis_index("gy")
    nx, ny, nz = out.shape
    used = [0]

    def here(dx, dy):
        x, y = mx + dx, my + dy
        ok = jnp.bool_(True)
        if dx:
            ok = jnp.logical_and(ok, jnp.logical_and(x >= 0, x < gx))
        if dy:
            ok = jnp.logical_and(ok, jnp.logical_and(y >= 0, y < gy))
        return ok, {"gx": x, "gy": y}

    def exchange(src, src_at, dst, dst_at, n, low, high, offsets):
        copies = []
        for dx, dy in offsets:
            fx, tx, cx = cut(n[0], dx, low, high)
            fy, ty, cy = cut(n[1], dy, low, high)
            ok, target = here(dx, dy)
            copy = pltpu.make_async_remote_copy(
                src_ref=src.at[pl.ds(src_at[0] + fx, cx), pl.ds(src_at[1] + fy, cy), :],
                dst_ref=dst.at[pl.ds(dst_at[0] + tx, cx), pl.ds(dst_at[1] + ty, cy), :],
                send_sem=send_sem.at[used[0]],
                recv_sem=recv_sem.at[used[0]],
                device_id=target,
                device_id_type=MESH,
            )
            used[0] += 1
            pl.when(ok)(copy.start)
            copies.append((ok, here(-dx, -dy)[0], copy))

        def wait():
            for sent, received, copy in copies:
                pl.when(received)(copy.wait_recv)
                pl.when(sent)(copy.wait_send)

        return wait

    def first_of(position, reach, span, total):
        return jnp.clip(position - reach, 0, total - span)

    base_x, base_y = first_of(mx, REACH, win_x, gx), first_of(my, REACH, win_y, gy)
    slot_x, slot_y = mx - base_x, my - base_y
    many_x = win_x if win_x == gx else 2 * win_x - 1
    many_y = win_y if win_y == gy else 2 * win_y - 1

    def partners(act):
        def one(index, carry):
            ix, iy = index // many_y, index % many_y
            tx = ix if win_x == gx else mx + ix - (win_x - 1)
            ty = iy if win_y == gy else my + iy - (win_y - 1)
            sends = (tx != mx) | (ty != my)
            takes = sends
            near_x, near_y, there_x, there_y = tx - base_x, ty - base_y, slot_x, slot_y
            if win_x != gx:
                there_x = mx - first_of(tx, REACH, win_x, gx)
                inside = (tx >= 0) & (tx < gx)
                sends = sends & inside & (there_x >= 0) & (there_x < win_x)
                takes = takes & inside & (near_x >= 0) & (near_x < win_x)
            if win_y != gy:
                there_y = my - first_of(ty, REACH, win_y, gy)
                inside = (ty >= 0) & (ty < gy)
                sends = sends & inside & (there_y >= 0) & (there_y < win_y)
                takes = takes & inside & (near_y >= 0) & (near_y < win_y)
            act((ix, iy), {"gx": tx, "gy": ty}, (near_x, near_y), (there_x, there_y), sends, takes)
            return carry + jnp.where(sends | takes, 1, 0)

        return lax.fori_loop(0, many_x * many_y, one, jnp.int32(0))

    def gather_copy(buffer, ssem, rsem, index, target, slot):
        return pltpu.make_async_remote_copy(
            src_ref=buffer.at[slot_x, slot_y],
            dst_ref=buffer.at[slot[0], slot[1]],
            send_sem=ssem.at[index[0], index[1]],
            recv_sem=rsem.at[slot[0], slot[1]],
            device_id=target,
            device_id_type=MESH,
        )

    def gather_start(buffer, ssem, rsem):
        def act(index, target, near, there, sends, takes):
            pl.when(sends)(gather_copy(buffer, ssem, rsem, index, target, there).start)

        partners(act)

    def gather_wait(buffer, ssem, rsem):
        def act(index, target, near, there, sends, takes):
            pl.when(takes)(gather_copy(buffer, ssem, rsem, index, target, near).wait_recv)
            pl.when(sends)(gather_copy(buffer, ssem, rsem, index, target, there).wait_send)

        partners(act)

    def parity(shape, offset):
        axes = [lax.broadcasted_iota(jnp.int32, shape, d) for d in range(3)]
        return (axes[0] + axes[1] + axes[2] + offset) & 1

    def vertical(v):
        k = lax.broadcasted_iota(jnp.int32, v.shape, 2)
        above = jnp.where(k == nz - 1, 0.0, pltpu.roll(v, nz - 1, 2))
        below = jnp.where(k == 0, 0.0, pltpu.roll(v, 1, 2))
        return above + below

    def flat(v):
        rows = v.shape[1]
        zero = jnp.zeros_like(v[:1])
        return (
            jnp.concatenate([v[1:], zero], axis=0)
            + jnp.concatenate([zero, v[:-1]], axis=0)
            + pltpu.roll(v, rows - 1, 1)
            + pltpu.roll(v, 1, 1)
        )

    def flat_of(ref, x, y, cx, cy):
        return (
            ref[x + 1 : x + 1 + cx, y : y + cy]
            + ref[x - 1 : x - 1 + cx, y : y + cy]
            + ref[x : x + cx, y + 1 : y + 1 + cy]
            + ref[x : x + cx, y - 1 : y - 1 + cy]
        )

    lanes = [(h, slice(128 * h, 128 * h + 128)) for h in range(nz // 128)]

    def put(buffer, i, rows, row):
        for h, lane in lanes:
            buffer[h, pl.ds(i, 1), rows] = row[None, :, lane]

    def every_other(buffer, count, y, rows):
        return jnp.concatenate(
            [buffer[h, :count, pl.ds(y, rows, stride=2)] for h, _ in lanes], axis=-1
        )

    def whole(buffer):
        return jnp.concatenate([buffer[h] for h, _ in lanes], axis=-1)

    def lift(buffer, i, y, row):
        for twice in range(2):
            for start_y in (y, y + 1):
                put(buffer, i + twice, pl.ds(start_y, row.shape[0], stride=2), row)

    for ref in (pot, start, first, delta, inv1, src1, inv2, src2, inv3, src3, e3, lift1, lift2):
        ref[...] = jnp.zeros(ref.shape, ref.dtype)
    reg[...] = jnp.ones(reg.shape, reg.dtype)

    barrier = pltpu.get_barrier_semaphore()

    def greet(index, target, near, there, sends, takes):
        @pl.when(sends | takes)
        def _():
            pl.semaphore_signal(barrier, inc=1, device_id=target, device_id_type=MESH)

    peers = partners(greet)
    if win_x == gx and win_y == gy:
        peers = gx * gy - 1

    p = potential[...]
    ids = region[...]
    movable = ids == 0
    dirichlet = jnp.zeros(p.shape, jnp.float32)
    for electrode in range(volts.shape[0]):
        dirichlet = jnp.where(ids == electrode + 1, volts[electrode], dirichlet)
    start[1 : nx + 1, 8 : ny + 8] = dirichlet
    pot[1 : nx + 1, 8 : ny + 8] = p
    reg[1 : nx + 1, 8 : ny + 8] = ids

    pl.semaphore_wait(barrier, peers)

    full = (nx, ny)
    wait_pot = exchange(potential, (0, 0), pot, (1, 8), full, 1, 1, FACES)
    wait_start = exchange(start, (1, 8), start, (1, 8), full, 1, 1, FACES)
    wait_reg = exchange(region, (0, 0), reg, (1, 8), full, 1, 0, LOW_FACES)

    bend = 0.5 * jnp.exp(p)
    inverse = 1.0 / (6.0 + bend)

    def coarsened(values, buffer):
        half_x, rows = values.shape[0] // 2, values.shape[1] // 2
        for i in range(half_x):
            put(buffer, i, slice(0, 2 * rows), 0.5 * (values[2 * i] + values[2 * i + 1]))
        return 0.5 * (every_other(buffer, half_x, 0, rows) + every_other(buffer, half_x, 1, rows))

    n1, n2, n3 = (nx // 2, ny // 2), (nx // 4, ny // 4), (nx // 8, ny // 8)
    c1 = coarsened(bend, u0)
    inv1[3 : 3 + n1[0], 8 : 8 + n1[1]] = 1.0 / (3.0 + c1)
    c2 = coarsened(c1, u1)
    inv2[4 : 4 + n2[0], 4 : 4 + n2[1]] = 1.0 / (2.25 + c2)
    c3 = coarsened(c2, u2)
    gat_i[pl.ds(slot_x, 1), pl.ds(slot_y, 1)] = (1.0 / (2.0625 + c3))[None, None]

    wait_pot()
    source = (
        charge[...]
        - (6.0 * p - (flat_of(pot, 1, 8, nx, ny) + vertical(p)))
        - (bend - 0.5)
    )
    wait_start()
    color = parity((nx, ny, nz), 0)
    even = jnp.logical_and(movable, color == 0)
    odd = jnp.logical_and(movable, color == 1)

    e = start[1 : nx + 1, 8 : ny + 8]
    e = jnp.where(even, (source + flat_of(start, 1, 8, nx, ny) + vertical(e)) * inverse, e)
    first[1 : nx + 1, 8 : ny + 8] = e
    wait_e = exchange(first, (1, 8), first, (1, 8), full, 1, 1, FACES)
    wait_inv1 = exchange(inv1, (3, 8), inv1, (3, 8), n1, 3, 3, AROUND)
    wait_inv2 = exchange(inv2, (4, 4), inv2, (4, 4), n2, 4, 4, AROUND)
    gather_start(gat_i, gsend_i, grecv_i)
    up_down = vertical(e)
    wait_e()
    new = (source + flat_of(first, 1, 8, nx, ny) + up_down) * inverse
    delta[2 : nx + 2, 8 : ny + 8] = jnp.where(odd, new, 0.0)
    wait_delta = exchange(delta, (2, 8), delta, (2, 8), full, 2, 1, LOW_DEEP)
    wait_reg()
    wait_inv1()
    wait_inv2()
    wait_delta()

    def narrowed(r, x, y, count, rows, buffer):
        width = r.shape[1]
        for i in range(count):
            a = x + 2 * i
            put(buffer, i, slice(0, width), 0.25 * r[a] + 0.5 * r[a + 1] + 0.25 * r[a + 2])
        return (
            0.25 * every_other(buffer, count, y, rows)
            + 0.5 * every_other(buffer, count, y + 1, rows)
            + 0.25 * every_other(buffer, count, y + 2, rows)
        )

    r = flat_of(delta, 1, 7, nx + 1, ny + 1) + vertical(delta[1 : nx + 2, 7 : ny + 8])
    live = jnp.logical_and(reg[:, 7 : ny + 8] == 0, parity(r.shape, 0) == 0)
    r = jnp.where(live, r, 0.0)
    src1[3 : 3 + n1[0], 8 : 8 + n1[1]] = narrowed(r, 0, 0, n1[0], n1[1], u0)
    wait_src1 = exchange(src1, (3, 8), src1, (3, 8), n1, 3, 3, AROUND)
    wait_src1()

    def down(src, inv, weight, offset):
        inverse, source = inv[...], src[...]
        color = parity(inv.shape, offset)
        red = jnp.where(color == 0, source * inverse, 0.0)
        black = jnp.where(color == 1, (source + weight * flat(red) + vertical(red)) * inverse, 0.0)
        r = jnp.where(
            jnp.logical_and(color == 0, inverse > 0.0), weight * flat(black) + vertical(black), 0.0
        )
        return red + black, r

    def sweep(e, source, inverse, weight, color):
        for c in range(2):
            e = jnp.where(color == c, (source + weight * flat(e) + vertical(e)) * inverse, e)
        return e

    e1, r = down(src1, inv1, 0.25, 1)
    src2[4 : 4 + n2[0], 4 : 4 + n2[1]] = narrowed(r, 2, 7, n2[0], n2[1], u1)
    wait_src2 = exchange(src2, (4, 4), src2, (4, 4), n2, 4, 4, AROUND)
    gather_wait(gat_i, gsend_i, grecv_i)
    for ix in range(win_x):
        for iy in range(win_y):
            inv3[2 * ix : 2 * ix + 2, 8 + 2 * iy : 10 + 2 * iy] = gat_i[ix, iy]
    wait_src2()
    e2, r = down(src2, inv2, 0.0625, 0)
    gat_s[pl.ds(slot_x, 1), pl.ds(slot_y, 1)] = narrowed(r, 3, 3, n3[0], n3[1], u2)[None, None]
    gather_start(gat_s, gsend_s, grecv_s)
    gather_wait(gat_s, gsend_s, grecv_s)
    for ix in range(win_x):
        for iy in range(win_y):
            src3[2 * ix : 2 * ix + 2, 8 + 2 * iy : 10 + 2 * iy] = gat_s[ix, iy]

    span3 = 2 * win_x
    color = parity(inv3.shape, 0)
    e3[2 : 2 + span3] = jnp.where(color == 0, src3[...] * inv3[...], 0.0)
    e = e3[2 : 2 + span3]
    e = jnp.where(
        color == 1, (src3[...] + 0.015625 * flat(e) + vertical(e)) * inv3[...], e
    )
    e3[2 : 2 + span3] = e

    def again(index, carry):
        e3[2 : 2 + span3] = sweep(e3[2 : 2 + span3], src3[...], inv3[...], 0.015625, parity(inv3.shape, 0))
        return carry

    lax.fori_loop(1, COARSE_SWEEPS, again, 0)

    for i in range(n3[0] + 4):
        row = e3[pl.ds(2 * slot_x + i, 1)]
        row = pltpu.roll(row, e3.shape[1] - 2 * slot_y, 1)[0, 6 : 10 + n3[1]]
        lift(lift2, 2 * i, 0, row)
    e2 = sweep(e2 + whole(lift2), src2[...], inv2[...], 0.0625, parity(inv2.shape, 0))
    for i in range(n2[0] + 2):
        lift(lift1, 1 + 2 * i, 6, e2[3 + i, 3 : 5 + n2[1]])
    e1 = sweep(e1 + whole(lift1), src1[...], inv1[...], 0.25, parity(inv1.shape, 1))
    for i in range(n1[0]):
        lift(u0, 2 * i, 0, e1[3 + i, 8 : 8 + n1[1]])
    e = first[1 : nx + 1, 8 : ny + 8] + delta[2 : nx + 2, 8 : ny + 8]
    e = e + jnp.where(movable, whole(u0)[:, :ny], 0.0)
    for buffer, chosen in ((start, even), (pot, odd)):
        buffer[1 : nx + 1, 8 : ny + 8] = e
        wait_up = exchange(buffer, (1, 8), buffer, (1, 8), full, 1, 1, FACES)
        up_down = vertical(e)
        wait_up()
        e = jnp.where(chosen, (source + flat_of(buffer, 1, 8, nx, ny) + up_down) * inverse, e)
    out[...] = e


def solution(mesh):
    gx, gy = mesh.shape["gx"], mesh.shape["gy"]
    win_x, win_y = min(gx, 2 * REACH + 1), min(gy, 2 * REACH + 1)
    many_x = win_x if win_x == gx else 2 * win_x - 1
    many_y = win_y if win_y == gy else 2 * win_y - 1

    def body(potential, charge, region, volts):
        nx, ny, nz = potential.shape
        f32 = jnp.float32

        def room(x, y, kind=f32):
            return pltpu.VMEM((x, y, nz), kind)

        def halves(x, y):
            return pltpu.VMEM((nz // 128, x, y, 128), f32)

        rows3 = -(-(2 * win_y + 16) // 8) * 8
        scratch = [
            room(nx + 2, ny + 16),
            room(nx + 2, ny + 16),
            room(nx + 2, ny + 16),
            room(nx + 3, ny + 16),
            room(nx + 1, ny + 8, jnp.int32),
            room(nx // 2 + 6, ny // 2 + 16),
            room(nx // 2 + 6, ny // 2 + 16),
            room(nx // 4 + 8, ny // 4 + 12),
            room(nx // 4 + 8, ny // 4 + 12),
            pltpu.VMEM((win_x, win_y, nx // 8, ny // 8, nz), f32),
            pltpu.VMEM((win_x, win_y, nx // 8, ny // 8, nz), f32),
            room(2 * win_x, rows3),
            room(2 * win_x, rows3),
            room(2 * win_x + 4, rows3),
            halves(nx // 4 + 8, ny // 4 + 12),
            halves(nx // 2 + 6, ny // 2 + 16),
            halves(nx, ny + 8),
            halves(nx // 2, ny // 2 + 16),
            halves(nx // 4, ny // 4 + 12),
            pltpu.SemaphoreType.DMA((64,)),
            pltpu.SemaphoreType.DMA((64,)),
            pltpu.SemaphoreType.DMA((many_x, many_y)),
            pltpu.SemaphoreType.DMA((win_x, win_y)),
            pltpu.SemaphoreType.DMA((many_x, many_y)),
            pltpu.SemaphoreType.DMA((win_x, win_y)),
        ]
        return pl.pallas_call(
            functools.partial(kernel, gx, gy, win_x, win_y),
            out_shape=jax.ShapeDtypeStruct(potential.shape, f32),
            in_specs=[pl.BlockSpec(memory_space=pltpu.VMEM)] * 3 + [pl.BlockSpec(memory_space=pltpu.SMEM)],
            out_specs=pl.BlockSpec(memory_space=pltpu.VMEM),
            scratch_shapes=scratch,
            compiler_params=pltpu.CompilerParams(
                collective_id=0, has_side_effects=True, vmem_limit_bytes=48 * 1024 * 1024
            ),
        )(potential, charge, region, volts)

    placed = (P("gx", "gy", None), P("gx", "gy", None), P("gx", "gy", None), P())
    return jax.shard_map(
        body, mesh=mesh, in_specs=placed, out_specs=P("gx", "gy", None), check_vma=False
    )
```

time: 400 us -> 48.9 us (0.12); the launches traced: 393 us -> 48.7 us
  starting transfers between devices: 305 us -> 0 us
  waiting for transfers between devices: 66 us -> 0 us
  Pallas kernels: 0 us -> 44.5 us
  other arithmetic: 16.5 us -> 0 us
    ppermute x102 -> x0, starting transfers between devices: 305 us -> none  [the longest x48 204 us: extended(): lax.ppermute(lax.slice_in_dim(block, block.shape[dim] - width, None, axis...]
    ppermute x102 -> x0, waiting for transfers between devices: 66 us -> none  [the longest x48 50 us: extended(): lax.ppermute(lax.slice_in_dim(block, 0, width, axis=dim), axis, backward)]
    pallas_call x0 -> x1, Pallas kernels: none -> 44.5 us  [body(): pl.pallas_call(functools.partial(kernel, gx, gy, win_x, win_y), out_shape...]
    add x11 -> x0, other arithmetic: 11.5 us -> none  [the longest x1 11.3 us: body(): dirichlet + jnp.where(region == electrode + 1, electrode_volts[electrode]...]
    select_n x21 -> x0, other arithmetic: 4.23 us -> none  [the longest x20 3.98 us: half_sweep(): return jnp.where(update, renewed, iterate)]
    unnamed x11 -> x9, local copies, waits for them, and re-layouts: 0.06 us -> 4.21 us
  transfers between devices with their start and end apart: 102 -> 0, of which waited for: 39 -> 0; matrix products, arithmetic and copies ran while one was open for 1% -> 0% of each run, Pallas kernels for 0% -> 0%
where the time goes in v1:
time: 48.9 us; the launch traced here: 48.7 us
  Pallas kernels  44.5 us (91%)
  local copies, waits for them, and re-layouts  4.21 us (9%)
    pallas_call x1, Pallas kernels, body(): pl.pallas_call(functools.partial(kernel, gx, gy, win_x, win_y), out_shape...  44.5 us
    unnamed x9, local copies, waits for them, and re-layouts  4.21 us

profile of v1, /device:TPU:1, one launch (start us, length us, event | category | flops | bytes accessed | tf_op | source)
XLA Modules:
  0.0 48.7 jit_solution(17931078242182416884)
XLA Ops:
  0.0 0.0 copy-start
  0.0 0.9 %copy-done = f32[16,16,256]{2,1,0:T(8,128)S(1)} copy-done((f32[16,16,256]{2,1,0:T(8,128)S(1)}, f32[16,16,256]{2,1,0:T(8,128)}, u32[]{:S(2)}) %copy-start) | copy-done | bytes 262168
  1.0 0.0 copy-start.1
  1.0 0.9 %copy-done.1 = f32[16,16,256]{2,1,0:T(8,128)S(1)} copy-done((f32[16,16,256]{2,1,0:T(8,128)S(1)}, f32[16,16,256]{2,1,0:T(8,128)}, u32[]{:S(2)}) %copy-start.1) | copy-done | bytes 262168
  1.9 0.0 copy-start.2
  1.9 0.9 %copy-done.2 = s32[16,16,256]{2,1,0:T(8,128)S(1)} copy-done((s32[16,16,256]{2,1,0:T(8,128)S(1)}, s32[16,16,256]{2,1,0:T(8,128)}, u32[]{:S(2)}) %copy-start.2) | copy-done | bytes 262168
  2.9 0.0 copy-start.3
  2.9 0.7 %copy-done.3 = f32[16]{0:T(128)S(1)} copy-done((f32[16]{0:T(128)S(1)}, f32[16]{0:T(128)}, u32[]{:S(2)}) %copy-start.3) | copy-done | bytes 88
  3.5 44.5 %shard_map.46 = f32[16,16,256]{2,1,0:T(8,128)S(1)} custom-call(f32[16,16,256]{2,1,0:T(8,128)S(1)} %copy-done, f32[16,16,256]{2,1,0:T(8,128)S(1)} %copy-done.1, s32[16,16,256]{2,1,0:T(8,128)S(1)} %copy-done.2, f32[16]{0:T(128)S(1)} %copy-done.3), custom_call_target="tpu_custom_call" | custom-call | tf_op jit(solution)/shard_map/pallas_call | solution.py:376
  48.0 0.7 %copy.6 = f32[16,16,256]{2,1,0:T(8,128)} copy(f32[16,16,256]{2,1,0:T(8,128)S(1)} %shard_map.46) | data formatting | bytes 524288
Async XLA Ops:
  0.0 0.9 %copy-start = (f32[16,16,256]{2,1,0:T(8,128)S(1)}, f32[16,16,256]{2,1,0:T(8,128)}, u32[]{:S(2)}) copy-start(f32[16,16,256]{2,1,0:T(8,128)} %potential.1) | copy-start | bytes 786436
  1.0 0.9 %copy-start.1 = (f32[16,16,256]{2,1,0:T(8,128)S(1)}, f32[16,16,256]{2,1,0:T(8,128)}, u32[]{:S(2)}) copy-start(f32[16,16,256]{2,1,0:T(8,128)} %charge.1) | copy-start | bytes 786436
  1.9 0.9 %copy-start.2 = (s32[16,16,256]{2,1,0:T(8,128)S(1)}, s32[16,16,256]{2,1,0:T(8,128)}, u32[]{:S(2)}) copy-start(s32[16,16,256]{2,1,0:T(8,128)} %region.1) | copy-start | bytes 786436
  2.9 0.7 %copy-start.3 = (f32[16]{0:T(128)S(1)}, f32[16]{0:T(128)}, u32[]{:S(2)}) copy-start(f32[16]{0:T(128)} %volts.1) | copy-start | bytes 196

commit v2 on v1

--- a/solution.py
+++ b/solution.py
@@ -26,7 +26,7 @@
     gx, gy, win_x, win_y,
     potential, charge, region, volts, out,
     pot, start, first, delta, reg, inv1, src1, inv2, src2, gat_i, gat_s, inv3, src3, e3, lift2, lift1, u0, u1, u2,
-    send_sem, recv_sem, gsend_i, grecv_i, gsend_s, grecv_s,
+    send_sem, recv_sem, gsend_i, grecv_i, gsend_s, grecv_s, charges, volt, in_sem,
 ):
     mx, my = lax.axis_index("gx"), lax.axis_index("gy")
     nx, ny, nz = out.shape
@@ -95,7 +95,11 @@
             act((ix, iy), {"gx": tx, "gy": ty}, (near_x, near_y), (there_x, there_y), sends, takes)
             return carry + jnp.where(sends | takes, 1, 0)
 
-        return lax.fori_loop(0, many_x * many_y, one, jnp.int32(0))
+        if many_x * many_y > 64:
+            return lax.fori_loop(0, many_x * many_y, one, jnp.int32(0))
+        for index in range(many_x * many_y):
+            one(index, 0)
+        return None
 
     def gather_copy(buffer, ssem, rsem, index, target, slot):
         return pltpu.make_async_remote_copy(
@@ -167,9 +171,23 @@
             for start_y in (y, y + 1):
                 put(buffer, i + twice, pl.ds(start_y, row.shape[0], stride=2), row)
 
-    for ref in (pot, start, first, delta, inv1, src1, inv2, src2, inv3, src3, e3, lift1, lift2):
+    pot[...] = jnp.zeros(pot.shape, jnp.float32)
+    reg[...] = jnp.ones(reg.shape, jnp.int32)
+    loads = [
+        pltpu.make_async_copy(source, target, in_sem.at[index])
+        for index, (source, target) in enumerate(
+            (
+                (region, reg.at[1 : nx + 1, 8 : ny + 8]),
+                (potential, pot.at[1 : nx + 1, 8 : ny + 8]),
+                (charge, charges),
+                (volts, volt),
+            )
+        )
+    ]
+    for load in loads:
+        load.start()
+    for ref in (start, first, delta, inv1, src1, inv2, src2, inv3, src3, e3, lift1, lift2):
         ref[...] = jnp.zeros(ref.shape, ref.dtype)
-    reg[...] = jnp.ones(reg.shape, reg.dtype)
 
     barrier = pltpu.get_barrier_semaphore()
 
@@ -182,22 +200,22 @@
     if win_x == gx and win_y == gy:
         peers = gx * gy - 1
 
-    p = potential[...]
-    ids = region[...]
+    for load in loads:
+        load.wait()
+    p = pot[1 : nx + 1, 8 : ny + 8]
+    ids = reg[1 : nx + 1, 8 : ny + 8]
     movable = ids == 0
     dirichlet = jnp.zeros(p.shape, jnp.float32)
     for electrode in range(volts.shape[0]):
-        dirichlet = jnp.where(ids == electrode + 1, volts[electrode], dirichlet)
+        dirichlet = jnp.where(ids == electrode + 1, volt[electrode], dirichlet)
     start[1 : nx + 1, 8 : ny + 8] = dirichlet
-    pot[1 : nx + 1, 8 : ny + 8] = p
-    reg[1 : nx + 1, 8 : ny + 8] = ids
 
     pl.semaphore_wait(barrier, peers)
 
     full = (nx, ny)
-    wait_pot = exchange(potential, (0, 0), pot, (1, 8), full, 1, 1, FACES)
+    wait_pot = exchange(pot, (1, 8), pot, (1, 8), full, 1, 1, FACES)
     wait_start = exchange(start, (1, 8), start, (1, 8), full, 1, 1, FACES)
-    wait_reg = exchange(region, (0, 0), reg, (1, 8), full, 1, 0, LOW_FACES)
+    wait_reg = exchange(reg, (1, 8), reg, (1, 8), full, 1, 0, LOW_FACES)
 
     bend = 0.5 * jnp.exp(p)
     inverse = 1.0 / (6.0 + bend)
@@ -218,7 +236,7 @@
 
     wait_pot()
     source = (
-        charge[...]
+        charges[...]
         - (6.0 * p - (flat_of(pot, 1, 8, nx, ny) + vertical(p)))
         - (bend - 0.5)
     )
@@ -372,15 +390,18 @@
             pltpu.SemaphoreType.DMA((win_x, win_y)),
             pltpu.SemaphoreType.DMA((many_x, many_y)),
             pltpu.SemaphoreType.DMA((win_x, win_y)),
+            room(nx, ny),
+            pltpu.SMEM(volts.shape, f32),
+            pltpu.SemaphoreType.DMA((4,)),
         ]
         return pl.pallas_call(
             functools.partial(kernel, gx, gy, win_x, win_y),
             out_shape=jax.ShapeDtypeStruct(potential.shape, f32),
-            in_specs=[pl.BlockSpec(memory_space=pltpu.VMEM)] * 3 + [pl.BlockSpec(memory_space=pltpu.SMEM)],
+            in_specs=[pl.BlockSpec(memory_space=pl.ANY)] * 4,
             out_specs=pl.BlockSpec(memory_space=pltpu.VMEM),
             scratch_shapes=scratch,
             compiler_params=pltpu.CompilerParams(
-                collective_id=0, has_side_effects=True, vmem_limit_bytes=48 * 1024 * 1024
+                collective_id=0, has_side_effects=True, vmem_limit_bytes=60 * 1024 * 1024
             ),
         )(potential, charge, region, volts)
 

time: 48.9 us -> 46 us (0.941)
  local copies, waits for them, and re-layouts: 4.21 us -> 1.67 us
    unnamed x9 -> x1, local copies, waits for them, and re-layouts: 4.21 us -> 1.67 us
where the time goes in v2:
time: 46 us; the launch traced here: 45.9 us
  Pallas kernels  44.2 us (96%)
  local copies, waits for them, and re-layouts  1.67 us (4%)
    pallas_call x1, Pallas kernels, body(): pl.pallas_call(functools.partial(kernel, gx, gy, win_x, win_y), out_shape...  44.2 us
    unnamed x1, local copies, waits for them, and re-layouts  1.67 us

profile of v2, /device:TPU:1, one launch (start us, length us, event | category | flops | bytes accessed | tf_op | source)
XLA Modules:
  0.0 45.9 jit_solution(16353570282440535265)
XLA Ops:
  0.0 44.2 %shard_map.46 = f32[16,16,256]{2,1,0:T(8,128)} custom-call(f32[16,16,256]{2,1,0:T(8,128)} %potential.1, f32[16,16,256]{2,1,0:T(8,128)} %charge.1, s32[16,16,256]{2,1,0:T(8,128)} %region.1, f32[16]{0:T(128)} %volts.1), custom_call_target="tpu_custom_call" | custom-call | tf_op jit(solution)/shard_map/pallas_call | solution.py:397
  44.2 1.7 %copy.6 = f32[16,16,256]{2,1,0:T(8,128)} copy(f32[16,16,256]{2,1,0:T(8,128)} %shard_map.46) | data formatting | bytes 524288

commit v3 on v2

--- a/solution.py
+++ b/solution.py
@@ -13,8 +13,8 @@
 
 FACES = ((1, 0), (-1, 0), (0, 1), (0, -1))
 AROUND = FACES + ((1, 1), (1, -1), (-1, 1), (-1, -1))
-LOW_FACES = ((1, 0), (0, 1), (1, 1))
-LOW_DEEP = FACES + ((1, 1), (1, -1), (-1, 1))
+NEAR = tuple((x, y) for x in range(-2, 3) for y in range(-2, 3) if x or y)
+FREE = 1e30
 
 
 def cut(n, d, low, high):
@@ -25,8 +25,8 @@
 def kernel(
     gx, gy, win_x, win_y,
     potential, charge, region, volts, out,
-    pot, start, first, delta, reg, inv1, src1, inv2, src2, gat_i, gat_s, inv3, src3, e3, lift2, lift1, u0, u1, u2,
-    send_sem, recv_sem, gsend_i, grecv_i, gsend_s, grecv_s, charges, volt, in_sem,
+    pot, code, chg, delta, start, first, source_rim, inverse_rim, ids, inv1, src1, inv2, src2, gat_i, gat_s, inv3, src3, e3, lift2, lift1, u0, u1, u2,
+    send_sem, recv_sem, gsend_i, grecv_i, gsend_s, grecv_s, volt, in_sem,
 ):
     mx, my = lax.axis_index("gx"), lax.axis_index("gy")
     nx, ny, nz = out.shape
@@ -49,7 +49,7 @@
             ok, target = here(dx, dy)
             copy = pltpu.make_async_remote_copy(
                 src_ref=src.at[pl.ds(src_at[0] + fx, cx), pl.ds(src_at[1] + fy, cy), :],
-                dst_ref=dst.at[pl.ds(dst_at[0] + tx, cx), pl.ds(dst_at[1] + ty, cy), :],
+                dst_ref=dst.at[pl.ds(dst_at[0] + tx, cx), pl.ds((dst_at[1] + ty) % dst.shape[1], cy), :],
                 send_sem=send_sem.at[used[0]],
                 recv_sem=recv_sem.at[used[0]],
                 device_id=target,
@@ -171,22 +171,24 @@
             for start_y in (y, y + 1):
                 put(buffer, i + twice, pl.ds(start_y, row.shape[0], stride=2), row)
 
-    pot[...] = jnp.zeros(pot.shape, jnp.float32)
-    reg[...] = jnp.ones(reg.shape, jnp.int32)
+    for ref in (pot, chg):
+        ref[...] = jnp.zeros(ref.shape, jnp.float32)
+    own = (slice(2, nx + 2), slice(8, ny + 8))
+    rim = (slice(1, nx + 3), slice(7, ny + 9))
     loads = [
         pltpu.make_async_copy(source, target, in_sem.at[index])
         for index, (source, target) in enumerate(
             (
-                (region, reg.at[1 : nx + 1, 8 : ny + 8]),
-                (potential, pot.at[1 : nx + 1, 8 : ny + 8]),
-                (charge, charges),
                 (volts, volt),
+                (region, ids),
+                (potential, pot.at[own[0], own[1]]),
+                (charge, chg.at[own[0], own[1]]),
             )
         )
     ]
     for load in loads:
         load.start()
-    for ref in (start, first, delta, inv1, src1, inv2, src2, inv3, src3, e3, lift1, lift2):
+    for ref in (code, delta, inv1, src1, inv2, src2, inv3, src3, e3, lift1, lift2):
         ref[...] = jnp.zeros(ref.shape, ref.dtype)
 
     barrier = pltpu.get_barrier_semaphore()
@@ -202,23 +204,19 @@
 
     for load in loads:
         load.wait()
-    p = pot[1 : nx + 1, 8 : ny + 8]
-    ids = reg[1 : nx + 1, 8 : ny + 8]
-    movable = ids == 0
-    dirichlet = jnp.zeros(p.shape, jnp.float32)
+    coded = jnp.full((nx, ny, nz), FREE, jnp.float32)
     for electrode in range(volts.shape[0]):
-        dirichlet = jnp.where(ids == electrode + 1, volt[electrode], dirichlet)
-    start[1 : nx + 1, 8 : ny + 8] = dirichlet
+        coded = jnp.where(ids[...] == electrode + 1, volt[electrode], coded)
+    code[own] = coded
 
     pl.semaphore_wait(barrier, peers)
 
     full = (nx, ny)
-    wait_pot = exchange(pot, (1, 8), pot, (1, 8), full, 1, 1, FACES)
-    wait_start = exchange(start, (1, 8), start, (1, 8), full, 1, 1, FACES)
-    wait_reg = exchange(reg, (1, 8), reg, (1, 8), full, 1, 0, LOW_FACES)
-
-    bend = 0.5 * jnp.exp(p)
-    inverse = 1.0 / (6.0 + bend)
+    wait_code = exchange(code, (2, 8), code, (2, 8), full, 2, 2, AROUND)
+    wait_pot = exchange(pot, (2, 8), pot, (2, 8), full, 2, 2, AROUND)
+    wait_chg = exchange(chg, (2, 8), chg, (2, 8), full, 1, 1, AROUND)
+
+    bend = 0.5 * jnp.exp(pot[own])
 
     def coarsened(values, buffer):
         half_x, rows = values.shape[0] // 2, values.shape[1] // 2
@@ -228,36 +226,47 @@
 
     n1, n2, n3 = (nx // 2, ny // 2), (nx // 4, ny // 4), (nx // 8, ny // 8)
     c1 = coarsened(bend, u0)
-    inv1[3 : 3 + n1[0], 8 : 8 + n1[1]] = 1.0 / (3.0 + c1)
+    inv1[4 : 4 + n1[0], 8 : 8 + n1[1]] = 1.0 / (3.0 + c1)
     c2 = coarsened(c1, u1)
-    inv2[4 : 4 + n2[0], 4 : 4 + n2[1]] = 1.0 / (2.25 + c2)
+    inv2[5 : 5 + n2[0], 4 : 4 + n2[1]] = 1.0 / (2.25 + c2)
     c3 = coarsened(c2, u2)
     gat_i[pl.ds(slot_x, 1), pl.ds(slot_y, 1)] = (1.0 / (2.0625 + c3))[None, None]
 
+    wait_code()
     wait_pot()
+    wait_chg()
+    wait_inv1 = exchange(inv1, (4, 8), inv1, (4, 8), n1, 4, 4, AROUND)
+    wait_inv2 = exchange(inv2, (5, 4), inv2, (5, 4), n2, 5, 5, NEAR)
+    gather_start(gat_i, gsend_i, grecv_i)
+    coded = code[...]
+    start[...] = jnp.where(coded == FREE, 0.0, coded)
+
+    p = pot[rim]
+    bend = 0.5 * jnp.exp(p)
+    inverse = 1.0 / (6.0 + bend)
     source = (
-        charges[...]
-        - (6.0 * p - (flat_of(pot, 1, 8, nx, ny) + vertical(p)))
+        chg[rim]
+        - (6.0 * p - (flat_of(pot, 1, 7, nx + 2, ny + 2) + vertical(p)))
         - (bend - 0.5)
     )
-    wait_start()
-    color = parity((nx, ny, nz), 0)
+    movable = code[rim] == FREE
+    color = parity(p.shape, 0)
     even = jnp.logical_and(movable, color == 0)
-    odd = jnp.logical_and(movable, color == 1)
-
-    e = start[1 : nx + 1, 8 : ny + 8]
-    e = jnp.where(even, (source + flat_of(start, 1, 8, nx, ny) + vertical(e)) * inverse, e)
-    first[1 : nx + 1, 8 : ny + 8] = e
-    wait_e = exchange(first, (1, 8), first, (1, 8), full, 1, 1, FACES)
-    wait_inv1 = exchange(inv1, (3, 8), inv1, (3, 8), n1, 3, 3, AROUND)
-    wait_inv2 = exchange(inv2, (4, 4), inv2, (4, 4), n2, 4, 4, AROUND)
-    gather_start(gat_i, gsend_i, grecv_i)
-    up_down = vertical(e)
-    wait_e()
-    new = (source + flat_of(first, 1, 8, nx, ny) + up_down) * inverse
-    delta[2 : nx + 2, 8 : ny + 8] = jnp.where(odd, new, 0.0)
-    wait_delta = exchange(delta, (2, 8), delta, (2, 8), full, 2, 1, LOW_DEEP)
-    wait_reg()
+    e = start[rim]
+    e = jnp.where(even, (source + flat_of(start, 1, 7, nx + 2, ny + 2) + vertical(e)) * inverse, e)
+    first[rim] = e
+    inverse_rim[...] = inverse
+    source_rim[...] = source
+    inner = (slice(1, nx + 1), slice(1, ny + 1))
+
+    def odd_half(buffer):
+        return (
+            source_rim[inner] + flat_of(buffer, 2, 8, nx, ny) + vertical(buffer[own])
+        ) * inverse_rim[inner]
+
+    odd = jnp.logical_and(code[own] == FREE, parity((nx, ny, nz), 0) == 1)
+    delta[own] = jnp.where(odd, odd_half(first), 0.0)
+    wait_delta = exchange(delta, (2, 8), delta, (2, 8), full, 2, 2, AROUND)
     wait_inv1()
     wait_inv2()
     wait_delta()
@@ -274,10 +283,10 @@
         )
 
     r = flat_of(delta, 1, 7, nx + 1, ny + 1) + vertical(delta[1 : nx + 2, 7 : ny + 8])
-    live = jnp.logical_and(reg[:, 7 : ny + 8] == 0, parity(r.shape, 0) == 0)
+    live = jnp.logical_and(code[1 : nx + 2, 7 : ny + 8] == FREE, parity(r.shape, 0) == 0)
     r = jnp.where(live, r, 0.0)
-    src1[3 : 3 + n1[0], 8 : 8 + n1[1]] = narrowed(r, 0, 0, n1[0], n1[1], u0)
-    wait_src1 = exchange(src1, (3, 8), src1, (3, 8), n1, 3, 3, AROUND)
+    src1[4 : 4 + n1[0], 8 : 8 + n1[1]] = narrowed(r, 0, 0, n1[0], n1[1], u0)
+    wait_src1 = exchange(src1, (4, 8), src1, (4, 8), n1, 4, 4, AROUND)
     wait_src1()
 
     def down(src, inv, weight, offset):
@@ -288,23 +297,23 @@
         r = jnp.where(
             jnp.logical_and(color == 0, inverse > 0.0), weight * flat(black) + vertical(black), 0.0
         )
-        return red + black, r
+        return black, r
 
     def sweep(e, source, inverse, weight, color):
         for c in range(2):
             e = jnp.where(color == c, (source + weight * flat(e) + vertical(e)) * inverse, e)
         return e
 
-    e1, r = down(src1, inv1, 0.25, 1)
-    src2[4 : 4 + n2[0], 4 : 4 + n2[1]] = narrowed(r, 2, 7, n2[0], n2[1], u1)
-    wait_src2 = exchange(src2, (4, 4), src2, (4, 4), n2, 4, 4, AROUND)
+    e1, r = down(src1, inv1, 0.25, 0)
+    src2[5 : 5 + n2[0], 4 : 4 + n2[1]] = narrowed(r, 3, 7, n2[0], n2[1], u1)
+    wait_src2 = exchange(src2, (5, 4), src2, (5, 4), n2, 5, 5, NEAR)
     gather_wait(gat_i, gsend_i, grecv_i)
     for ix in range(win_x):
         for iy in range(win_y):
             inv3[2 * ix : 2 * ix + 2, 8 + 2 * iy : 10 + 2 * iy] = gat_i[ix, iy]
     wait_src2()
-    e2, r = down(src2, inv2, 0.0625, 0)
-    gat_s[pl.ds(slot_x, 1), pl.ds(slot_y, 1)] = narrowed(r, 3, 3, n3[0], n3[1], u2)[None, None]
+    e2, r = down(src2, inv2, 0.0625, 1)
+    gat_s[pl.ds(slot_x, 1), pl.ds(slot_y, 1)] = narrowed(r, 4, 3, n3[0], n3[1], u2)[None, None]
     gather_start(gat_s, gsend_s, grecv_s)
     gather_wait(gat_s, gsend_s, grecv_s)
     for ix in range(win_x):
@@ -329,22 +338,25 @@
     for i in range(n3[0] + 4):
         row = e3[pl.ds(2 * slot_x + i, 1)]
         row = pltpu.roll(row, e3.shape[1] - 2 * slot_y, 1)[0, 6 : 10 + n3[1]]
-        lift(lift2, 2 * i, 0, row)
-    e2 = sweep(e2 + whole(lift2), src2[...], inv2[...], 0.0625, parity(inv2.shape, 0))
-    for i in range(n2[0] + 2):
-        lift(lift1, 1 + 2 * i, 6, e2[3 + i, 3 : 5 + n2[1]])
-    e1 = sweep(e1 + whole(lift1), src1[...], inv1[...], 0.25, parity(inv1.shape, 1))
-    for i in range(n1[0]):
-        lift(u0, 2 * i, 0, e1[3 + i, 8 : 8 + n1[1]])
-    e = first[1 : nx + 1, 8 : ny + 8] + delta[2 : nx + 2, 8 : ny + 8]
-    e = e + jnp.where(movable, whole(u0)[:, :ny], 0.0)
-    for buffer, chosen in ((start, even), (pot, odd)):
-        buffer[1 : nx + 1, 8 : ny + 8] = e
-        wait_up = exchange(buffer, (1, 8), buffer, (1, 8), full, 1, 1, FACES)
-        up_down = vertical(e)
-        wait_up()
-        e = jnp.where(chosen, (source + flat_of(buffer, 1, 8, nx, ny) + up_down) * inverse, e)
-    out[...] = e
+        lift(lift2, 1 + 2 * i, 0, row)
+    e2 = sweep(e2 + whole(lift2), src2[...], inv2[...], 0.0625, parity(inv2.shape, 1))
+    for i in range(n2[0] + 4):
+        lift(lift1, 2 * i, 4, e2[3 + i, 2 : 6 + n2[1]])
+    e1 = sweep(e1 + whole(lift1), src1[...], inv1[...], 0.25, parity(inv1.shape, 0))
+    for i in range(n1[0] + 2):
+        lift(u0, 2 * i, 6, e1[3 + i, 7 : 9 + n1[1]])
+    coded = code[...]
+    start[...] = jnp.where(coded == FREE, delta[...] + whole(u0), coded)
+    even = jnp.logical_and(code[rim] == FREE, parity(source_rim.shape, 0) == 0)
+    e = start[rim]
+    e = jnp.where(
+        even,
+        (source_rim[...] + flat_of(start, 1, 7, nx + 2, ny + 2) + vertical(e)) * inverse_rim[...],
+        e,
+    )
+    first[rim] = e
+    odd = jnp.logical_and(code[own] == FREE, parity((nx, ny, nz), 0) == 1)
+    out[...] = jnp.where(odd, odd_half(first), first[own])
 
 
 def solution(mesh):
@@ -365,32 +377,27 @@
 
         rows3 = -(-(2 * win_y + 16) // 8) * 8
         scratch = [
-            room(nx + 2, ny + 16),
-            room(nx + 2, ny + 16),
-            room(nx + 2, ny + 16),
-            room(nx + 3, ny + 16),
-            room(nx + 1, ny + 8, jnp.int32),
-            room(nx // 2 + 6, ny // 2 + 16),
-            room(nx // 2 + 6, ny // 2 + 16),
-            room(nx // 4 + 8, ny // 4 + 12),
-            room(nx // 4 + 8, ny // 4 + 12),
+            *([room(nx + 4, ny + 16)] * 6),
+            *([room(nx + 2, ny + 2)] * 2),
+            room(nx, ny, jnp.int32),
+            *([room(nx // 2 + 8, ny // 2 + 16)] * 2),
+            *([room(nx // 4 + 10, ny // 4 + 12)] * 2),
             pltpu.VMEM((win_x, win_y, nx // 8, ny // 8, nz), f32),
             pltpu.VMEM((win_x, win_y, nx // 8, ny // 8, nz), f32),
             room(2 * win_x, rows3),
             room(2 * win_x, rows3),
             room(2 * win_x + 4, rows3),
-            halves(nx // 4 + 8, ny // 4 + 12),
-            halves(nx // 2 + 6, ny // 2 + 16),
-            halves(nx, ny + 8),
+            halves(nx // 4 + 10, ny // 4 + 12),
+            halves(nx // 2 + 8, ny // 2 + 16),
+            halves(nx + 4, ny + 16),
             halves(nx // 2, ny // 2 + 16),
             halves(nx // 4, ny // 4 + 12),
-            pltpu.SemaphoreType.DMA((64,)),
-            pltpu.SemaphoreType.DMA((64,)),
+            pltpu.SemaphoreType.DMA((96,)),
+            pltpu.SemaphoreType.DMA((96,)),
             pltpu.SemaphoreType.DMA((many_x, many_y)),
             pltpu.SemaphoreType.DMA((win_x, win_y)),
             pltpu.SemaphoreType.DMA((many_x, many_y)),
             pltpu.SemaphoreType.DMA((win_x, win_y)),
-            room(nx, ny),
             pltpu.SMEM(volts.shape, f32),
             pltpu.SemaphoreType.DMA((4,)),
         ]

time: 46 us -> 44.5 us (0.967)
  Pallas kernels: 44.2 us -> 42.6 us
    pallas_call x1, Pallas kernels: 44.2 us -> 42.6 us  [body(): pl.pallas_call(functools.partial(kernel, gx, gy, win_x, win_y), out_shape...]
where the time goes in v3:
time: 44.5 us; the launch traced here: 44.3 us
  Pallas kernels  42.6 us (96%)
  local copies, waits for them, and re-layouts  1.67 us (4%)
    pallas_call x1, Pallas kernels, body(): pl.pallas_call(functools.partial(kernel, gx, gy, win_x, win_y), out_shape...  42.6 us
    unnamed x1, local copies, waits for them, and re-layouts  1.67 us

profile of v3, /device:TPU:1, one launch (start us, length us, event | category | flops | bytes accessed | tf_op | source)
XLA Modules:
  0.0 44.3 jit_solution(4844762322004528940)
XLA Ops:
  0.0 42.6 %shard_map.46 = f32[16,16,256]{2,1,0:T(8,128)} custom-call(f32[16,16,256]{2,1,0:T(8,128)} %potential.1, f32[16,16,256]{2,1,0:T(8,128)} %charge.1, s32[16,16,256]{2,1,0:T(8,128)} %region.1, f32[16]{0:T(128)} %volts.1), custom_call_target="tpu_custom_call" | custom-call | tf_op jit(solution)/shard_map/pallas_call | solution.py:404
  42.7 1.7 %copy.6 = f32[16,16,256]{2,1,0:T(8,128)} copy(f32[16,16,256]{2,1,0:T(8,128)} %shard_map.46) | data formatting | bytes 524288

commit v4 on v3

--- a/solution.py
+++ b/solution.py
@@ -25,7 +25,7 @@
 def kernel(
     gx, gy, win_x, win_y,
     potential, charge, region, volts, out,
-    pot, code, chg, delta, start, first, source_rim, inverse_rim, ids, inv1, src1, inv2, src2, gat_i, gat_s, inv3, src3, e3, lift2, lift1, u0, u1, u2,
+    pot, code, chg, delta, source, red_inv, black_inv, ids, inv1, src1, inv2, src2, gat_i, gat_s, inv3, src3, e3, lift2, lift1, u0, u1, u2,
     send_sem, recv_sem, gsend_i, grecv_i, gsend_s, grecv_s, volt, in_sem,
 ):
     mx, my = lax.axis_index("gx"), lax.axis_index("gy")
@@ -129,28 +129,34 @@
         return (axes[0] + axes[1] + axes[2] + offset) & 1
 
     def vertical(v):
-        k = lax.broadcasted_iota(jnp.int32, v.shape, 2)
-        above = jnp.where(k == nz - 1, 0.0, pltpu.roll(v, nz - 1, 2))
-        below = jnp.where(k == 0, 0.0, pltpu.roll(v, 1, 2))
-        return above + below
-
-    def flat(v):
+        parts = [v[..., 128 * h : 128 * h + 128] for h in range(nz // 128)]
+        lane = lax.broadcasted_iota(jnp.int32, parts[0].shape, 2)
+        zero = jnp.zeros_like(parts[0])
+        ups = [pltpu.roll(part, 127, 2) for part in parts] + [zero]
+        downs = [zero] + [pltpu.roll(part, 1, 2) for part in parts]
+        return jnp.concatenate(
+            [
+                jnp.where(lane == 127, ups[h + 1], ups[h]) + jnp.where(lane == 0, downs[h], downs[h + 1])
+                for h in range(len(parts))
+            ],
+            axis=-1,
+        )
+
+    def around(v, weight, walled=False):
         rows = v.shape[1]
         zero = jnp.zeros_like(v[:1])
-        return (
+        above, below = pltpu.roll(v, rows - 1, 1), pltpu.roll(v, 1, 1)
+        if walled:
+            row = lax.broadcasted_iota(jnp.int32, v.shape, 1)
+            above = jnp.where(row == rows - 1, 0.0, above)
+            below = jnp.where(row == 0, 0.0, below)
+        flat = (
             jnp.concatenate([v[1:], zero], axis=0)
             + jnp.concatenate([zero, v[:-1]], axis=0)
-            + pltpu.roll(v, rows - 1, 1)
-            + pltpu.roll(v, 1, 1)
-        )
-
-    def flat_of(ref, x, y, cx, cy):
-        return (
-            ref[x + 1 : x + 1 + cx, y : y + cy]
-            + ref[x - 1 : x - 1 + cx, y : y + cy]
-            + ref[x : x + cx, y + 1 : y + 1 + cy]
-            + ref[x : x + cx, y - 1 : y - 1 + cy]
-        )
+            + above
+            + below
+        )
+        return weight * flat + vertical(v)
 
     lanes = [(h, slice(128 * h, 128 * h + 128)) for h in range(nz // 128)]
 
@@ -166,18 +172,21 @@
     def whole(buffer):
         return jnp.concatenate([buffer[h] for h, _ in lanes], axis=-1)
 
-    def lift(buffer, i, y, row):
+    def lift(buffer, i, low, high):
         for twice in range(2):
-            for start_y in (y, y + 1):
-                put(buffer, i + twice, pl.ds(start_y, row.shape[0], stride=2), row)
+            for y in range(2):
+                for rows, first in ((low, buffer.shape[2] - 2 * low.shape[0]), (high, 0)):
+                    if rows.shape[0] == 1:
+                        put(buffer, i + twice, pl.ds(first + y, 1), rows)
+                    else:
+                        put(buffer, i + twice, pl.ds(first + y, rows.shape[0], stride=2), rows)
 
     for ref in (pot, chg):
         ref[...] = jnp.zeros(ref.shape, jnp.float32)
-    own = (slice(2, nx + 2), slice(8, ny + 8))
-    rim = (slice(1, nx + 3), slice(7, ny + 9))
+    own = (slice(2, nx + 2), slice(0, ny))
     loads = [
-        pltpu.make_async_copy(source, target, in_sem.at[index])
-        for index, (source, target) in enumerate(
+        pltpu.make_async_copy(origin, target, in_sem.at[index])
+        for index, (origin, target) in enumerate(
             (
                 (volts, volt),
                 (region, ids),
@@ -212,9 +221,9 @@
     pl.semaphore_wait(barrier, peers)
 
     full = (nx, ny)
-    wait_code = exchange(code, (2, 8), code, (2, 8), full, 2, 2, AROUND)
-    wait_pot = exchange(pot, (2, 8), pot, (2, 8), full, 2, 2, AROUND)
-    wait_chg = exchange(chg, (2, 8), chg, (2, 8), full, 1, 1, AROUND)
+    wait_code = exchange(code, (2, 0), code, (2, 0), full, 2, 2, AROUND)
+    wait_pot = exchange(pot, (2, 0), pot, (2, 0), full, 2, 2, AROUND)
+    wait_chg = exchange(chg, (2, 0), chg, (2, 0), full, 1, 1, AROUND)
 
     bend = 0.5 * jnp.exp(pot[own])
 
@@ -226,137 +235,110 @@
 
     n1, n2, n3 = (nx // 2, ny // 2), (nx // 4, ny // 4), (nx // 8, ny // 8)
     c1 = coarsened(bend, u0)
-    inv1[4 : 4 + n1[0], 8 : 8 + n1[1]] = 1.0 / (3.0 + c1)
+    inv1[4 : 4 + n1[0], : n1[1]] = 1.0 / (3.0 + c1)
     c2 = coarsened(c1, u1)
-    inv2[5 : 5 + n2[0], 4 : 4 + n2[1]] = 1.0 / (2.25 + c2)
+    inv2[5 : 5 + n2[0], : n2[1]] = 1.0 / (2.25 + c2)
     c3 = coarsened(c2, u2)
     gat_i[pl.ds(slot_x, 1), pl.ds(slot_y, 1)] = (1.0 / (2.0625 + c3))[None, None]
 
     wait_code()
     wait_pot()
     wait_chg()
-    wait_inv1 = exchange(inv1, (4, 8), inv1, (4, 8), n1, 4, 4, AROUND)
-    wait_inv2 = exchange(inv2, (5, 4), inv2, (5, 4), n2, 5, 5, NEAR)
+    wait_inv1 = exchange(inv1, (4, 0), inv1, (4, 0), n1, 4, 4, AROUND)
+    wait_inv2 = exchange(inv2, (5, 0), inv2, (5, 0), n2, 5, 5, NEAR)
     gather_start(gat_i, gsend_i, grecv_i)
-    coded = code[...]
-    start[...] = jnp.where(coded == FREE, 0.0, coded)
-
-    p = pot[rim]
+
+    def split(inverse, offset, live=None):
+        if live is not None:
+            inverse = jnp.where(live, inverse, 0.0)
+        color = parity(inverse.shape, offset)
+        return jnp.where(color == 0, inverse, 0.0), jnp.where(color == 0, 0.0, inverse)
+
+    p, coded = pot[...], code[...]
+    free = coded == FREE
     bend = 0.5 * jnp.exp(p)
-    inverse = 1.0 / (6.0 + bend)
-    source = (
-        chg[rim]
-        - (6.0 * p - (flat_of(pot, 1, 7, nx + 2, ny + 2) + vertical(p)))
-        - (bend - 0.5)
+    red_inv[...], black_inv[...] = split(1.0 / (6.0 + bend), 0, free)
+    source[...] = (
+        chg[...] - 6.0 * p + around(p + jnp.where(free, 0.0, coded), 1.0) - (bend - 0.5)
     )
-    movable = code[rim] == FREE
-    color = parity(p.shape, 0)
-    even = jnp.logical_and(movable, color == 0)
-    e = start[rim]
-    e = jnp.where(even, (source + flat_of(start, 1, 7, nx + 2, ny + 2) + vertical(e)) * inverse, e)
-    first[rim] = e
-    inverse_rim[...] = inverse
-    source_rim[...] = source
-    inner = (slice(1, nx + 1), slice(1, ny + 1))
-
-    def odd_half(buffer):
-        return (
-            source_rim[inner] + flat_of(buffer, 2, 8, nx, ny) + vertical(buffer[own])
-        ) * inverse_rim[inner]
-
-    odd = jnp.logical_and(code[own] == FREE, parity((nx, ny, nz), 0) == 1)
-    delta[own] = jnp.where(odd, odd_half(first), 0.0)
-    wait_delta = exchange(delta, (2, 8), delta, (2, 8), full, 2, 2, AROUND)
+    red = source[...] * red_inv[...]
+    mid = slice(2, nx + 2)
+    rows = slice(0, ny)
+    delta[own] = ((source[...] + around(red, 1.0)) * black_inv[...])[mid, rows]
+    wait_delta = exchange(delta, (2, 0), delta, (2, 0), full, 2, 2, AROUND)
     wait_inv1()
     wait_inv2()
     wait_delta()
 
-    def narrowed(r, x, y, count, rows, buffer):
+    def narrowed(r, x, count, rows, buffer):
         width = r.shape[1]
         for i in range(count):
             a = x + 2 * i
-            put(buffer, i, slice(0, width), 0.25 * r[a] + 0.5 * r[a + 1] + 0.25 * r[a + 2])
+            plane = 0.25 * r[a : a + 1] + 0.5 * r[a + 1 : a + 2] + 0.25 * r[a + 2 : a + 3]
+            put(buffer, i, slice(0, width), pltpu.roll(plane, 1, 1)[0])
         return (
-            0.25 * every_other(buffer, count, y, rows)
-            + 0.5 * every_other(buffer, count, y + 1, rows)
-            + 0.25 * every_other(buffer, count, y + 2, rows)
-        )
-
-    r = flat_of(delta, 1, 7, nx + 1, ny + 1) + vertical(delta[1 : nx + 2, 7 : ny + 8])
-    live = jnp.logical_and(code[1 : nx + 2, 7 : ny + 8] == FREE, parity(r.shape, 0) == 0)
-    r = jnp.where(live, r, 0.0)
-    src1[4 : 4 + n1[0], 8 : 8 + n1[1]] = narrowed(r, 0, 0, n1[0], n1[1], u0)
-    wait_src1 = exchange(src1, (4, 8), src1, (4, 8), n1, 4, 4, AROUND)
+            0.25 * every_other(buffer, count, 0, rows)
+            + 0.5 * every_other(buffer, count, 1, rows)
+            + 0.25 * every_other(buffer, count, 2, rows)
+        )
+
+    r = jnp.where(red_inv[...] > 0.0, around(delta[...], 1.0), 0.0)
+    src1[4 : 4 + n1[0], : n1[1]] = narrowed(r, 1, n1[0], n1[1], u0)
+    wait_src1 = exchange(src1, (4, 0), src1, (4, 0), n1, 4, 4, AROUND)
+    inverses1 = split(inv1[...], 0)
     wait_src1()
 
-    def down(src, inv, weight, offset):
-        inverse, source = inv[...], src[...]
-        color = parity(inv.shape, offset)
-        red = jnp.where(color == 0, source * inverse, 0.0)
-        black = jnp.where(color == 1, (source + weight * flat(red) + vertical(red)) * inverse, 0.0)
-        r = jnp.where(
-            jnp.logical_and(color == 0, inverse > 0.0), weight * flat(black) + vertical(black), 0.0
-        )
-        return black, r
-
-    def sweep(e, source, inverse, weight, color):
-        for c in range(2):
-            e = jnp.where(color == c, (source + weight * flat(e) + vertical(e)) * inverse, e)
-        return e
-
-    e1, r = down(src1, inv1, 0.25, 0)
-    src2[5 : 5 + n2[0], 4 : 4 + n2[1]] = narrowed(r, 3, 7, n2[0], n2[1], u1)
-    wait_src2 = exchange(src2, (5, 4), src2, (5, 4), n2, 5, 5, NEAR)
+    def down(source, inverses, weight):
+        red = source * inverses[0]
+        black = (source + around(red, weight)) * inverses[1]
+        return black, jnp.where(inverses[0] > 0.0, around(black, weight), 0.0)
+
+    def up(black, source, inverses, weight):
+        red = (source + around(black, weight)) * inverses[0]
+        return red + (source + around(red, weight)) * inverses[1]
+
+    black1, r = down(src1[...], inverses1, 0.25)
+    src2[5 : 5 + n2[0], : n2[1]] = narrowed(r, 3, n2[0], n2[1], u1)
+    wait_src2 = exchange(src2, (5, 0), src2, (5, 0), n2, 5, 5, NEAR)
+    inverses2 = split(inv2[...], 1)
     gather_wait(gat_i, gsend_i, grecv_i)
     for ix in range(win_x):
         for iy in range(win_y):
-            inv3[2 * ix : 2 * ix + 2, 8 + 2 * iy : 10 + 2 * iy] = gat_i[ix, iy]
+            inv3[2 * ix : 2 * ix + 2, 2 * iy : 2 * iy + 2] = gat_i[ix, iy]
+    inverses3 = split(inv3[...], 0)
     wait_src2()
-    e2, r = down(src2, inv2, 0.0625, 1)
-    gat_s[pl.ds(slot_x, 1), pl.ds(slot_y, 1)] = narrowed(r, 4, 3, n3[0], n3[1], u2)[None, None]
+    black2, r = down(src2[...], inverses2, 0.0625)
+    gat_s[pl.ds(slot_x, 1), pl.ds(slot_y, 1)] = narrowed(r, 4, n3[0], n3[1], u2)[None, None]
     gather_start(gat_s, gsend_s, grecv_s)
     gather_wait(gat_s, gsend_s, grecv_s)
     for ix in range(win_x):
         for iy in range(win_y):
-            src3[2 * ix : 2 * ix + 2, 8 + 2 * iy : 10 + 2 * iy] = gat_s[ix, iy]
-
-    span3 = 2 * win_x
-    color = parity(inv3.shape, 0)
-    e3[2 : 2 + span3] = jnp.where(color == 0, src3[...] * inv3[...], 0.0)
-    e = e3[2 : 2 + span3]
-    e = jnp.where(
-        color == 1, (src3[...] + 0.015625 * flat(e) + vertical(e)) * inv3[...], e
-    )
-    e3[2 : 2 + span3] = e
-
-    def again(index, carry):
-        e3[2 : 2 + span3] = sweep(e3[2 : 2 + span3], src3[...], inv3[...], 0.015625, parity(inv3.shape, 0))
-        return carry
-
-    lax.fori_loop(1, COARSE_SWEEPS, again, 0)
+            src3[2 * ix : 2 * ix + 2, 2 * iy : 2 * iy + 2] = gat_s[ix, iy]
+
+    def renewed(other, inverse):
+        return (src3[...] + around(other, 0.015625, walled=True)) * inverse
+
+    red = src3[...] * inverses3[0]
+    for _ in range(COARSE_SWEEPS - 1):
+        red = renewed(renewed(red, inverses3[1]), inverses3[0])
+    e3[2 : 2 + 2 * win_x, 8 : 8 + src3.shape[1]] = red + renewed(red, inverses3[1])
 
     for i in range(n3[0] + 4):
         row = e3[pl.ds(2 * slot_x + i, 1)]
-        row = pltpu.roll(row, e3.shape[1] - 2 * slot_y, 1)[0, 6 : 10 + n3[1]]
-        lift(lift2, 1 + 2 * i, 0, row)
-    e2 = sweep(e2 + whole(lift2), src2[...], inv2[...], 0.0625, parity(inv2.shape, 1))
+        row = pltpu.roll(row, e3.shape[1] - 2 * slot_y, 1)[0]
+        lift(lift2, 1 + 2 * i, row[6:8], row[8 : 10 + n3[1]])
+    e2 = up(
+        black2 + whole(lift2), src2[...], inverses2, 0.0625
+    )
     for i in range(n2[0] + 4):
-        lift(lift1, 2 * i, 4, e2[3 + i, 2 : 6 + n2[1]])
-    e1 = sweep(e1 + whole(lift1), src1[...], inv1[...], 0.25, parity(inv1.shape, 0))
+        lift(lift1, 2 * i, e2[3 + i, -2:], e2[3 + i, : 2 + n2[1]])
+    e1 = up(black1 + whole(lift1), src1[...], inverses1, 0.25)
     for i in range(n1[0] + 2):
-        lift(u0, 2 * i, 6, e1[3 + i, 7 : 9 + n1[1]])
+        lift(u0, 2 * i, e1[3 + i, -1:], e1[3 + i, : 1 + n1[1]])
     coded = code[...]
-    start[...] = jnp.where(coded == FREE, delta[...] + whole(u0), coded)
-    even = jnp.logical_and(code[rim] == FREE, parity(source_rim.shape, 0) == 0)
-    e = start[rim]
-    e = jnp.where(
-        even,
-        (source_rim[...] + flat_of(start, 1, 7, nx + 2, ny + 2) + vertical(e)) * inverse_rim[...],
-        e,
-    )
-    first[rim] = e
-    odd = jnp.logical_and(code[own] == FREE, parity((nx, ny, nz), 0) == 1)
-    out[...] = jnp.where(odd, odd_half(first), first[own])
+    black = jnp.where(coded == FREE, delta[...] + whole(u0), 0.0)
+    e = up(black, source[...], (red_inv[...], black_inv[...]), 1.0)
+    out[...] = e[mid, rows] + jnp.where(coded == FREE, 0.0, coded)[mid, rows]
 
 
 def solution(mesh):
@@ -375,21 +357,20 @@
         def halves(x, y):
             return pltpu.VMEM((nz // 128, x, y, 128), f32)
 
-        rows3 = -(-(2 * win_y + 16) // 8) * 8
+        rows3 = -(-2 * win_y // 8) * 8
         scratch = [
-            *([room(nx + 4, ny + 16)] * 6),
-            *([room(nx + 2, ny + 2)] * 2),
+            *([room(nx + 4, ny + 8)] * 7),
             room(nx, ny, jnp.int32),
-            *([room(nx // 2 + 8, ny // 2 + 16)] * 2),
+            *([room(nx // 2 + 8, ny // 2 + 8)] * 2),
             *([room(nx // 4 + 10, ny // 4 + 12)] * 2),
             pltpu.VMEM((win_x, win_y, nx // 8, ny // 8, nz), f32),
             pltpu.VMEM((win_x, win_y, nx // 8, ny // 8, nz), f32),
             room(2 * win_x, rows3),
             room(2 * win_x, rows3),
-            room(2 * win_x + 4, rows3),
+            room(2 * win_x + 4, rows3 + 16),
             halves(nx // 4 + 10, ny // 4 + 12),
-            halves(nx // 2 + 8, ny // 2 + 16),
-            halves(nx + 4, ny + 16),
+            halves(nx // 2 + 8, ny // 2 + 8),
+            halves(nx + 4, ny + 8),
             halves(nx // 2, ny // 2 + 16),
             halves(nx // 4, ny // 4 + 12),
             pltpu.SemaphoreType.DMA((96,)),

time: 44.5 us -> 42.6 us (0.957)
  Pallas kernels: 42.6 us -> 40.8 us
    pallas_call x1, Pallas kernels: 42.6 us -> 40.8 us  [body(): pl.pallas_call(functools.partial(kernel, gx, gy, win_x, win_y), out_shape...]
where the time goes in v4:
time: 42.6 us; the launch traced here: 42.5 us
  Pallas kernels  40.8 us (96%)
  local copies, waits for them, and re-layouts  1.67 us (4%)
    pallas_call x1, Pallas kernels, body(): pl.pallas_call(functools.partial(kernel, gx, gy, win_x, win_y), out_shape...  40.8 us
    unnamed x1, local copies, waits for them, and re-layouts  1.67 us

profile of v4, /device:TPU:1, one launch (start us, length us, event | category | flops | bytes accessed | tf_op | source)
XLA Modules:
  0.0 42.5 jit_solution(7362039598978464738)
XLA Ops:
  0.0 40.8 %shard_map.46 = f32[16,16,256]{2,1,0:T(8,128)} custom-call(f32[16,16,256]{2,1,0:T(8,128)} %potential.1, f32[16,16,256]{2,1,0:T(8,128)} %charge.1, s32[16,16,256]{2,1,0:T(8,128)} %region.1, f32[16]{0:T(128)} %volts.1), custom_call_target="tpu_custom_call" | custom-call | tf_op jit(solution)/shard_map/pallas_call | solution.py:385
  40.8 1.7 %copy.6 = f32[16,16,256]{2,1,0:T(8,128)} copy(f32[16,16,256]{2,1,0:T(8,128)} %shard_map.46) | data formatting | bytes 524288

commit v5 on v4

--- a/solution.py
+++ b/solution.py
@@ -241,12 +241,12 @@
     c3 = coarsened(c2, u2)
     gat_i[pl.ds(slot_x, 1), pl.ds(slot_y, 1)] = (1.0 / (2.0625 + c3))[None, None]
 
+    wait_inv1 = exchange(inv1, (4, 0), inv1, (4, 0), n1, 4, 4, AROUND)
+    wait_inv2 = exchange(inv2, (5, 0), inv2, (5, 0), n2, 5, 5, NEAR)
+    gather_start(gat_i, gsend_i, grecv_i)
     wait_code()
     wait_pot()
     wait_chg()
-    wait_inv1 = exchange(inv1, (4, 0), inv1, (4, 0), n1, 4, 4, AROUND)
-    wait_inv2 = exchange(inv2, (5, 0), inv2, (5, 0), n2, 5, 5, NEAR)
-    gather_start(gat_i, gsend_i, grecv_i)
 
     def split(inverse, offset, live=None):
         if live is not None:
@@ -266,8 +266,6 @@
     rows = slice(0, ny)
     delta[own] = ((source[...] + around(red, 1.0)) * black_inv[...])[mid, rows]
     wait_delta = exchange(delta, (2, 0), delta, (2, 0), full, 2, 2, AROUND)
-    wait_inv1()
-    wait_inv2()
     wait_delta()
 
     def narrowed(r, x, count, rows, buffer):
@@ -285,6 +283,7 @@
     r = jnp.where(red_inv[...] > 0.0, around(delta[...], 1.0), 0.0)
     src1[4 : 4 + n1[0], : n1[1]] = narrowed(r, 1, n1[0], n1[1], u0)
     wait_src1 = exchange(src1, (4, 0), src1, (4, 0), n1, 4, 4, AROUND)
+    wait_inv1()
     inverses1 = split(inv1[...], 0)
     wait_src1()
 
@@ -300,6 +299,7 @@
     black1, r = down(src1[...], inverses1, 0.25)
     src2[5 : 5 + n2[0], : n2[1]] = narrowed(r, 3, n2[0], n2[1], u1)
     wait_src2 = exchange(src2, (5, 0), src2, (5, 0), n2, 5, 5, NEAR)
+    wait_inv2()
     inverses2 = split(inv2[...], 1)
     gather_wait(gat_i, gsend_i, grecv_i)
     for ix in range(win_x):
@@ -385,11 +385,11 @@
         return pl.pallas_call(
             functools.partial(kernel, gx, gy, win_x, win_y),
             out_shape=jax.ShapeDtypeStruct(potential.shape, f32),
-            in_specs=[pl.BlockSpec(memory_space=pl.ANY)] * 4,
+            in_specs=[pl.BlockSpec(memory_space=pltpu.HBM)] * 4,
             out_specs=pl.BlockSpec(memory_space=pltpu.VMEM),
             scratch_shapes=scratch,
             compiler_params=pltpu.CompilerParams(
-                collective_id=0, has_side_effects=True, vmem_limit_bytes=60 * 1024 * 1024
+                collective_id=0, has_side_effects=True, vmem_limit_bytes=32 * 1024 * 1024
             ),
         )(potential, charge, region, volts)
 

time: 42.6 us -> 44.3 us (1.040)
  local copies, waits for them, and re-layouts: 1.67 us -> 4.21 us
  Pallas kernels: 40.8 us -> 39.9 us
    unnamed x1 -> x9, local copies, waits for them, and re-layouts: 1.67 us -> 4.21 us
    pallas_call x1, Pallas kernels: 40.8 us -> 39.9 us  [body(): pl.pallas_call(functools.partial(kernel, gx, gy, win_x, win_y), out_shape...]
where the time goes in v5:
time: 44.3 us; the launch traced here: 44.1 us
  Pallas kernels  39.9 us (90%)
  local copies, waits for them, and re-layouts  4.21 us (10%)
    pallas_call x1, Pallas kernels, body(): pl.pallas_call(functools.partial(kernel, gx, gy, win_x, win_y), out_shape...  39.9 us
    unnamed x9, local copies, waits for them, and re-layouts  4.21 us

profile of v5, /device:TPU:1, one launch (start us, length us, event | category | flops | bytes accessed | tf_op | source)
XLA Modules:
  0.0 44.1 jit_solution(11089426445560916270)
XLA Ops:
  0.0 0.0 copy-start
  0.0 0.9 %copy-done = f32[16,16,256]{2,1,0:T(8,128)S(1)} copy-done((f32[16,16,256]{2,1,0:T(8,128)S(1)}, f32[16,16,256]{2,1,0:T(8,128)}, u32[]{:S(2)}) %copy-start) | copy-done | bytes 262168
  1.0 0.0 copy-start.1
  1.0 0.9 %copy-done.1 = f32[16,16,256]{2,1,0:T(8,128)S(1)} copy-done((f32[16,16,256]{2,1,0:T(8,128)S(1)}, f32[16,16,256]{2,1,0:T(8,128)}, u32[]{:S(2)}) %copy-start.1) | copy-done | bytes 262168
  1.9 0.0 copy-start.2
  1.9 0.9 %copy-done.2 = s32[16,16,256]{2,1,0:T(8,128)S(1)} copy-done((s32[16,16,256]{2,1,0:T(8,128)S(1)}, s32[16,16,256]{2,1,0:T(8,128)}, u32[]{:S(2)}) %copy-start.2) | copy-done | bytes 262168
  2.9 0.0 copy-start.3
  2.9 0.7 %copy-done.3 = f32[16]{0:T(128)S(1)} copy-done((f32[16]{0:T(128)S(1)}, f32[16]{0:T(128)}, u32[]{:S(2)}) %copy-start.3) | copy-done | bytes 88
  3.5 39.9 %shard_map.46 = f32[16,16,256]{2,1,0:T(8,128)S(1)} custom-call(f32[16,16,256]{2,1,0:T(8,128)S(1)} %copy-done, f32[16,16,256]{2,1,0:T(8,128)S(1)} %copy-done.1, s32[16,16,256]{2,1,0:T(8,128)S(1)} %copy-done.2, f32[16]{0:T(128)S(1)} %copy-done.3), custom_call_target="tpu_custom_call" | custom-call | tf_op jit(solution)/shard_map/pallas_call | solution.py:385
  43.4 0.7 %copy.6 = f32[16,16,256]{2,1,0:T(8,128)} copy(f32[16,16,256]{2,1,0:T(8,128)S(1)} %shard_map.46) | data formatting | bytes 524288
Async XLA Ops:
  0.0 0.9 %copy-start = (f32[16,16,256]{2,1,0:T(8,128)S(1)}, f32[16,16,256]{2,1,0:T(8,128)}, u32[]{:S(2)}) copy-start(f32[16,16,256]{2,1,0:T(8,128)} %potential.1) | copy-start | bytes 786436
  1.0 0.9 %copy-start.1 = (f32[16,16,256]{2,1,0:T(8,128)S(1)}, f32[16,16,256]{2,1,0:T(8,128)}, u32[]{:S(2)}) copy-start(f32[16,16,256]{2,1,0:T(8,128)} %charge.1) | copy-start | bytes 786436
  1.9 0.9 %copy-start.2 = (s32[16,16,256]{2,1,0:T(8,128)S(1)}, s32[16,16,256]{2,1,0:T(8,128)}, u32[]{:S(2)}) copy-start(s32[16,16,256]{2,1,0:T(8,128)} %region.1) | copy-start | bytes 786436
  2.9 0.7 %copy-start.3 = (f32[16]{0:T(128)S(1)}, f32[16]{0:T(128)}, u32[]{:S(2)}) copy-start(f32[16]{0:T(128)} %volts.1) | copy-start | bytes 196

commit v6 on v5

--- a/solution.py
+++ b/solution.py
@@ -11,7 +11,7 @@
 COARSE_SWEEPS = 4
 REACH = 5
 
-FACES = ((1, 0), (-1, 0), (0, 1), (0, -1))
+FACES = ((0, 1), (0, -1), (1, 0), (-1, 0))
 AROUND = FACES + ((1, 1), (1, -1), (-1, 1), (-1, -1))
 NEAR = tuple((x, y) for x in range(-2, 3) for y in range(-2, 3) if x or y)
 FREE = 1e30
@@ -385,11 +385,11 @@
         return pl.pallas_call(
             functools.partial(kernel, gx, gy, win_x, win_y),
             out_shape=jax.ShapeDtypeStruct(potential.shape, f32),
-            in_specs=[pl.BlockSpec(memory_space=pltpu.HBM)] * 4,
+            in_specs=[pl.BlockSpec(memory_space=pl.ANY)] * 4,
             out_specs=pl.BlockSpec(memory_space=pltpu.VMEM),
             scratch_shapes=scratch,
             compiler_params=pltpu.CompilerParams(
-                collective_id=0, has_side_effects=True, vmem_limit_bytes=32 * 1024 * 1024
+                collective_id=0, has_side_effects=True, vmem_limit_bytes=60 * 1024 * 1024
             ),
         )(potential, charge, region, volts)
 

time: 44.3 us -> 42.3 us (0.955)
  local copies, waits for them, and re-layouts: 4.21 us -> 1.67 us
  Pallas kernels: 39.9 us -> 40.5 us
    unnamed x9 -> x1, local copies, waits for them, and re-layouts: 4.21 us -> 1.67 us
    pallas_call x1, Pallas kernels: 39.9 us -> 40.5 us  [body(): pl.pallas_call(functools.partial(kernel, gx, gy, win_x, win_y), out_shape...]
where the time goes in v6:
time: 42.3 us; the launch traced here: 42.1 us
  Pallas kernels  40.5 us (96%)
  local copies, waits for them, and re-layouts  1.67 us (4%)
    pallas_call x1, Pallas kernels, body(): pl.pallas_call(functools.partial(kernel, gx, gy, win_x, win_y), out_shape...  40.5 us
    unnamed x1, local copies, waits for them, and re-layouts  1.67 us

profile of v6, /device:TPU:1, one launch (start us, length us, event | category | flops | bytes accessed | tf_op | source)
XLA Modules:
  0.0 42.1 jit_solution(6260995612805059830)
XLA Ops:
  0.0 40.5 %shard_map.46 = f32[16,16,256]{2,1,0:T(8,128)} custom-call(f32[16,16,256]{2,1,0:T(8,128)} %potential.1, f32[16,16,256]{2,1,0:T(8,128)} %charge.1, s32[16,16,256]{2,1,0:T(8,128)} %region.1, f32[16]{0:T(128)} %volts.1), custom_call_target="tpu_custom_call" | custom-call | tf_op jit(solution)/shard_map/pallas_call | solution.py:385
  40.5 1.7 %copy.6 = f32[16,16,256]{2,1,0:T(8,128)} copy(f32[16,16,256]{2,1,0:T(8,128)} %shard_map.46) | data formatting | bytes 524288
